TPU v7x, 256 devices: a whole 4x4x8 slice. The times are simulated.
256 devices in a mesh: tile: 64 (over y, z, core), head: 4 (over x).
Axes of the slice: x: 4, y: 4, z: 8, core: 2. Of those that a mesh axis runs over, the one named last changes fastest.
Arguments:
- obs_feat: bfloat16 [524288, 512], P('tile', 'head'), may hold values from -70 to 70, as said below
- row_valid: int32 [524288], P('tile'), may hold values 0 or 1
- block_owner: int32 [4096, 1], P('tile'), may hold values from 0 to 63; in each aligned block of 64 rows (0 to 63, 64 to 127, ...) at most 2 rows name the same one
- block_pattern: int32 [4096, 16], P('tile'), may hold values 0 or 1
- latent: bfloat16 [32768, 512], P('tile'), may hold values from -35 to 35, as said below
- w_query: bfloat16 [512, 512], P(None, 'head'), may hold values from -0.25 to 0.25
- w_key: bfloat16 [512, 512], P(None, 'head'), may hold values from -0.25 to 0.25
- w_value: bfloat16 [512, 512], P(None, 'head'), may hold values from -0.25 to 0.25
- self_bias: float32 [8], P('head'), may hold values from 2.5 to 4.5
- w_out: bfloat16 [512, 512], P('head'), may hold values from -0.25 to 0.25
- norm_gain: float32 [512], replicated, may hold values from 0.25 to 1.75
- w_inc: bfloat16 [512, 128], replicated, may hold values from -0.25 to 0.25
- target: bfloat16 [32768, 128], P('tile'), may hold values from -6 to 6
Outputs:
- increment: float32 [32768, 128], P('tile')
- head_gradient: float32 [512, 128], P('head')
Inputs may be any that keep to these rules, and one draw needn't show every extreme that they name: `obs_feat`: embedded features; rows may differ widely in scale. `latent`: latent state; rows may differ widely in scale. `block_owner`: among the 64 blocks of one shard, no tile is named by more than 2 blocks, a bound that some block reaches.
All inputs are finite; a program needn't handle non-finite values. No bound on the sum of `row_valid` or of `block_pattern` on one device may be relied on, other than what follows from the above.
Results may differ from a plain program's by a relative error of at most 0.0093.
Values may be sent and summed in bfloat16 or wider, within the bound.
No kernel may reach another device: no remote copies, remote signals or barrier semaphores. Data moves between devices by JAX's collectives and lax.ppermute only.
A program may use at most 128 MiB of HBM per device.

v0:
```python
import functools
import math

import jax
import jax.numpy as jnp
from jax import lax
from jax.experimental import pallas as pl
from jax.experimental.pallas import tpu as pltpu
from jax.sharding import PartitionSpec as P

BF = jnp.bfloat16
F32 = jnp.float32
NEG = -1e30
SLOTS = 2
CHUNK = 8
PAIR = 8
NEAR = (1, 16, 17, 48, 49, 2, 3, 32)
DEPTHS = (6, 6, 6, 6, 6, 6, 6, 2)


def route_kernel(spill, owner, alive, obs, row_marks, pattern, sent, info, lanes, extra, near):
    tiles = sent.shape[0]
    blocks, parts, quarter = obs.shape[:3]
    subs = pattern.shape[0]
    me = lax.axis_index("tile")
    lane = lax.broadcasted_iota(jnp.int32, (blocks, 128), 1)
    rows = row_marks[...].astype(F32)
    spot = lax.broadcasted_iota(jnp.int32, (subs, 128), 1)
    line = lax.broadcasted_iota(jnp.int32, (subs, 128), 0)
    shift = (spot == line + quarter).astype(F32).astype(BF)
    groups = lax.dot_general(
        pattern[...].astype(F32).astype(BF),
        shift,
        (((0,), (0,)), ((), ())),
        preferred_element_type=F32,
    )
    for j in range(parts):
        turned = rows if j == 0 else pltpu.roll(rows, 128 - j * quarter, 1)
        info[j, :blocks] = jnp.where(lane < quarter, turned, groups)
        info[j, blocks:] = jnp.zeros((8, 128), F32)
    for m, mask in enumerate(NEAR):
        near[m] = mask

    def clear(t, carry):
        lanes[t] = blocks
        lanes[tiles + t] = 0
        return carry

    lax.fori_loop(0, tiles, clear, 0, unroll=8)

    def place(b, n):
        t = owner[b]
        live = alive[b]
        seen = lanes[tiles + t]
        take = (live > 0) & ((seen == 0) if spill else (seen > 0))
        lanes[t] = jnp.where(take, b, lanes[t])
        lanes[tiles + t] = seen | live
        extra[n] = b
        return n + (live & seen)

    more = lax.fori_loop(0, blocks, place, jnp.int32(0), unroll=4)
    left = jnp.int32(0)
    if spill:

        def move(q, left):
            b = extra[q]
            t = owner[b]
            found = jnp.int32(tiles)
            last = len(NEAR) - 1
            for a in range(len(NEAR)):
                other = t ^ (NEAR[last] if a == last else near[(me + q + a) % last])
                free = (lanes[other] == blocks) & (found == tiles)
                found = jnp.where(free, other, found)

            @pl.when(found < tiles)
            def _():
                lanes[found] = b

            return left + (found == tiles).astype(jnp.int32)

        left = lax.fori_loop(0, more, move, left)

    lane1 = lax.broadcasted_iota(jnp.int32, (1, 128), 1)

    def goal(t):
        b = lanes[t]
        return jnp.where(b < blocks, owner[jnp.minimum(b, blocks - 1)] + 1, 0)

    def note(t, table):
        return jnp.where(lane1 == t, goal(t).astype(F32), table)

    table = jnp.where(lane1 == tiles, left.astype(F32), jnp.zeros((1, 128), F32))
    table = lax.fori_loop(0, tiles, note, table, unroll=8)
    line8 = lax.broadcasted_iota(jnp.int32, (8, 128), 0)

    def fill(t, carry):
        b = lanes[t]
        to = jnp.where(lane1 == quarter + subs, goal(t).astype(F32), 0.0)
        for j in range(parts):
            one = info[j, pl.ds(b, 1), :] + to
            tail = jnp.where(line8 == 0, one, jnp.where(line8 == 1, table, 0.0))
            sent[t, j, quarter:, :] = tail.astype(BF)

        @pl.when(b < blocks)
        def _():
            sent[t, :, :quarter, :] = obs[b]

        @pl.when(b >= blocks)
        def _():
            sent[t, :, :quarter, :] = jnp.zeros(obs.shape[1:], BF)

        return carry

    lax.fori_loop(0, tiles, fill, 0, unroll=2)


def prepare_kernel(*refs):
    biases, weights, (lat, qw, states, numer, wv, wo) = refs[:4], refs[4:8], refs[8:]
    me = lax.axis_index("head")
    heads, lat_rows, width = qw.shape
    each = heads // len(weights)
    size = width // heads
    scale = 1.0 / math.sqrt(size)
    latent = lat[...]
    lane = lax.broadcasted_iota(jnp.int32, (lat_rows, 128), 1)
    keep = jnp.where(me == 0, 1.0, 0.0)
    total = jnp.where((lane >= heads) & (lane < 2 * heads), keep, 0.0)
    for d, (bias, w) in enumerate(zip(biases, weights)):
        block = me ^ d
        far = pl.ds(pl.multiple_of(block * 128, 128), 128)
        q = jnp.dot(latent, w[:, :128], preferred_element_type=F32).astype(BF).astype(F32)
        k = jnp.dot(latent, w[:, 128:256], preferred_element_type=F32).astype(BF).astype(F32)
        v = jnp.dot(latent, w[:, 256:384], preferred_element_type=F32)
        numer[:, far] = v * keep
        wv[:, far] = w[:, 256:384]
        wo[:, far] = w[:, 384:]
        for e in range(each):
            mine = lane // size == e
            own = jnp.sum(jnp.where(mine, q * k, 0.0), axis=1, keepdims=True)
            own = own * scale + bias[e]
            total = jnp.where(lane == block * each + e, own, total)
            carried = lax.dot_general(
                jnp.where(mine, q, 0.0).astype(BF),
                w[:, 128:256],
                (((1,), (1,)), ((), ())),
                preferred_element_type=F32,
            )
            qw[block * each + e] = (carried * scale).astype(BF)
    states[...] = total


def before(n):
    return (
        lax.broadcasted_iota(jnp.int32, (n, n), 0) < lax.broadcasted_iota(jnp.int32, (n, n), 1)
    ).astype(F32).astype(BF)


def listing(live):
    rows, n = live.shape
    place = jnp.dot(live.astype(BF), before(n), preferred_element_type=F32)
    turn = lax.broadcasted_iota(jnp.int32, (rows, 128, n), 1).astype(F32)
    name = lax.broadcasted_iota(jnp.int32, (rows, 128, n), 2).astype(F32)
    hit = (place[:, None, :] == turn) & (live[:, None, :] > 0.5)
    order = jnp.sum(jnp.where(hit, name, 0.0), axis=2)
    return order, jnp.sum(live, axis=1, keepdims=True)


def plan_kernel(arrived, plan, *rest):
    *outs, lists, sem = rest
    tiles = arrived.shape[0]
    near = len(NEAR)
    me = lax.axis_index("tile")
    table = arrived[:, 0, 32:40, :].astype(F32)[:, 1, :]
    mine = (lax.broadcasted_iota(jnp.int32, (near, 128), 1) == me).astype(F32).astype(BF)
    goals = lax.dot_general(
        mine, table.astype(BF), (((1,), (1,)), ((), ())), preferred_element_type=F32
    )
    line = lax.broadcasted_iota(jnp.int32, (near, tiles), 0)
    want = jnp.zeros((near, tiles), jnp.int32)
    for m, mask in enumerate(NEAR):
        want = jnp.where(line == m, (me ^ mask) + 1, want)
    order, count = listing((goals == want.astype(F32)).astype(F32))
    place = lax.broadcasted_iota(jnp.int32, (near, 128), 1)
    plan[:near] = jnp.where(place.astype(F32) < count, order, tiles).astype(jnp.int32)
    lane = lax.broadcasted_iota(jnp.int32, (1, 128), 1)
    worst = jnp.zeros((1, 128), F32)
    for mask, depth in zip(NEAR, DEPTHS):
        here = (table == ((lane ^ mask) + 1).astype(F32)).astype(F32)
        total = jnp.sum(here, axis=0, keepdims=True)
        worst = jnp.maximum(worst, jnp.where(lane < tiles, total - depth, 0.0))
    left = jnp.sum(jnp.where(lane == tiles, table, 0.0), axis=0, keepdims=True)
    bad = jnp.max(jnp.where(worst > 0.0, 1.0, left), axis=1, keepdims=True)
    good = jnp.where(bad > 0.0, 0, 1)
    plan[near:] = jnp.broadcast_to(good, (near, 128))
    copy = pltpu.make_async_copy(plan, lists, sem)
    copy.start()
    copy.wait()
    for m, out in enumerate(outs):
        for c in range(DEPTHS[m]):
            s = lists[m, c]

            @pl.when(s < tiles)
            def _(s=s, out=out, c=c):
                out[c] = arrived[s]

            @pl.when(s >= tiles)
            def _(out=out, c=c):
                out[c] = jnp.zeros(out.shape[1:], BF)


def lists_of(marks, quarter, subs):
    me = lax.axis_index("tile")
    to = marks[:, quarter + subs:quarter + subs + 1]
    marks = jnp.where(to == (me + 1).astype(F32), marks, 0.0).astype(BF)
    pick_group = (
        lax.broadcasted_iota(jnp.int32, (subs, 128), 1)
        == lax.broadcasted_iota(jnp.int32, (subs, 128), 0) + quarter
    ).astype(F32).astype(BF)
    up = lax.broadcasted_iota(jnp.int32, (128, 128), 0)
    along = lax.broadcasted_iota(jnp.int32, (128, 128), 1)
    widen = ((up < quarter) & (up == along % quarter)).astype(F32).astype(BF)
    live = lax.dot_general(
        pick_group, marks, (((1,), (1,)), ((), ())), preferred_element_type=F32
    )
    order, count = listing(live)
    rows = jnp.dot(marks, widen, preferred_element_type=F32)
    return order, count, (rows - 1.0) * (-NEG)


def split3(v):
    hi = v.astype(BF).astype(F32)
    mid = (v - hi).astype(BF).astype(F32)
    return hi, mid, v - hi - mid


def attend_kernel(*refs):
    units = refs[:len(NEAR) + 2]
    qw, begun, given, wv, *refs = refs[len(NEAR) + 2:]
    outs, (x, sems, made, lists, bias, result, *scratch) = refs[:4], refs[4:]
    me = lax.axis_index("head")
    step_id = pl.program_id(0)
    quarter = 32

    @pl.when(step_id == 0)
    def _():
        copies = []
        at = 0
        for u, unit in enumerate(units):
            n = unit.shape[0]
            copies.append(pltpu.make_async_copy(unit, x.at[pl.ds(at, n)], sems.at[u]))
            at += n
        for copy in copies:
            copy.start()
        for copy in copies:
            copy.wait()
        marks = x[:, 0, quarter:quarter + 8, :].astype(F32)[:, 0, :]
        order, count, shade = lists_of(marks, quarter, made.shape[0])
        bias[...] = shade
        made[:, :128] = order.astype(jnp.int32)
        made[:, 128:] = jnp.broadcast_to(count, order.shape).astype(jnp.int32)
        copy = pltpu.make_async_copy(made, lists, sems.at[len(units)])
        copy.start()
        copy.wait()

    heads, both, width = qw.shape
    sub = both // PAIR
    rows = heads * sub
    parts, _, cols = x.shape[1:]
    size = CHUNK * quarter
    per = 128 // quarter
    lane_slot = lax.broadcasted_iota(jnp.int32, (1, 128), 1) // quarter
    lane = lax.broadcasted_iota(jnp.int32, (sub, 128), 1)
    xbufs, accs, tops, dens = (scratch[q * PAIR:(q + 1) * PAIR] for q in range(4))

    def gather(g, n, c, xbuf):
        shades = []
        for part in range(CHUNK // per):
            shade = jnp.full((1, 128), NEG, F32)
            for v in range(per):
                u = part * per + v
                place = c * CHUNK + u
                s = lists[g, jnp.maximum(jnp.minimum(place, n - 1), 0)]
                for i in range(parts):
                    xbuf[u * quarter:(u + 1) * quarter, i * cols:(i + 1) * cols] = x[
                        s, i, :quarter, :
                    ]
                live = (lane_slot == v) & (place < n)
                shade = jnp.where(live, bias[pl.ds(s, 1), :], shade)
            shades.append(shade)
        return xbuf[...], jnp.concatenate(shades, axis=1)

    def chunk(queries, rows_x, shade, old):
        scores = lax.dot_general(
            queries, rows_x, (((1,), (1,)), ((), ())), preferred_element_type=F32
        ) + shade
        new = jnp.maximum(old, jnp.max(scores, axis=1, keepdims=True))
        weights = jnp.exp(scores - jnp.concatenate([new] * (size // 128), axis=1))
        total = jnp.sum(weights, axis=1, keepdims=True)
        more = jnp.dot(weights.astype(BF), rows_x, preferred_element_type=F32)
        return new, jnp.exp(old - new), total, more

    counts, begins = [], []
    for p in range(PAIR):
        g = step_id * PAIR + p
        n = lists[g, 128]
        counts.append(n)
        start = begun[p * sub:(p + 1) * sub, :]
        old = jnp.concatenate(
            [jnp.broadcast_to(start[:, h:h + 1], (sub, 128)) for h in range(heads)], axis=0
        )
        den = jnp.concatenate(
            [
                jnp.broadcast_to(start[:, heads + h:heads + h + 1], (sub, 128))
                for h in range(heads)
            ],
            axis=0,
        )
        begins.append(old)
        rows_x, shade = gather(g, n, 0, xbufs[p])
        queries = qw[:, p * sub:(p + 1) * sub, :].reshape(rows, width)
        new, shrink, total, more = chunk(queries, rows_x, shade, old)
        accs[p][...] = more
        tops[p][...] = new
        dens[p][...] = den * shrink + total

    for p in range(PAIR):
        g = step_id * PAIR + p

        @pl.when(counts[p] > CHUNK)
        def _(p=p, g=g):
            def again(c, carry):
                rows_x, shade = gather(g, counts[p], c, xbufs[p])
                queries = qw[:, p * sub:(p + 1) * sub, :].reshape(rows, width)
                new, shrink, total, more = chunk(queries, rows_x, shade, tops[p][...])
                tops[p][...] = new
                dens[p][...] = dens[p][...] * shrink + total
                wide = jnp.concatenate([shrink] * (width // 128), axis=1)
                accs[p][...] = accs[p][...] * wide + more
                return carry

            lax.fori_loop(1, (counts[p] + CHUNK - 1) // CHUNK, again, 0)

    half = width // 2
    for p in range(PAIR):
        place = slice(p * sub, (p + 1) * sub)
        share = outs[0].shape[0]
        quarter_id = (step_id * (PAIR * sub // share) + p * sub // share) ^ me
        line0 = (p * sub) % share
        spot = slice(line0, line0 + sub)
        top = tops[p][...]
        shrink = jnp.exp(begins[p] - top)
        state = jnp.zeros((sub, 128), F32)
        for h in range(heads):
            line = slice(h * sub, (h + 1) * sub)
            state = jnp.where(lane == h, top[line], state)
            state = jnp.where(lane == heads + h, dens[p][line, :], state)
        hi, mid, lo = split3(state)
        packed = hi + pltpu.roll(mid, 2 * heads, 1) + pltpu.roll(lo, 4 * heads, 1)
        result[quarter_id, spot, width:] = packed.astype(BF)
        for side in range(2):
            here = slice(side * rows // 2, (side + 1) * rows // 2)
            mixed = jnp.dot(
                accs[p][here, :].astype(BF),
                wv[:, side * half:(side + 1) * half],
                preferred_element_type=F32,
            )
            for c in range(half // 128):
                col = side * half + c * 128
                two = []
                for h in (2 * c, 2 * c + 1):
                    line = slice(h * sub, (h + 1) * sub)
                    far = side * rows // 2
                    two.append(
                        given[place, col:col + 128] * shrink[far + h * sub:far + (h + 1) * sub]
                        + mixed[line, c * 128:(c + 1) * 128]
                    )
                result[quarter_id, spot, col:col + 128] = jnp.where(
                    lane < width // heads, two[0], two[1]
                ).astype(BF)

    @pl.when(step_id == pl.num_programs(0) - 1)
    def _():
        for d, out in enumerate(outs):
            out[...] = result[d]


def finish_kernel(place, r0, r1, r2, r3, lat, w_out, gain, w_inc, target, predicted, *grads):
    width = lat.shape[1]
    heads = 8
    line = lax.broadcasted_iota(jnp.int32, (128, 2 * width), 0)
    col = lax.broadcasted_iota(jnp.int32, (128, 2 * width), 1)
    match = (
        (line % heads == (col % width) // (width // heads))
        & ((line // heads) % 2 == col // width)
        & (line < 6 * heads)
    )
    spread = match.astype(F32).astype(BF)
    tops, dens, nums = [], [], []
    for r in (r0, r1, r2, r3):
        wide = jnp.dot(r[:, width:], spread, preferred_element_type=F32)
        tops.append(wide[:, :width])
        dens.append(wide[:, width:])
        nums.append(r[:, :width].astype(F32))
    best = jnp.maximum(jnp.maximum(tops[0], tops[1]), jnp.maximum(tops[2], tops[3]))
    scale = [jnp.exp(v - best) for v in tops]
    numer = sum(a * b for a, b in zip(scale, nums))
    denom = sum(a * b for a, b in zip(scale, dens))
    attended = (numer / denom).astype(BF)
    updated = lat[...].astype(F32) + lax.dot_general(
        attended, w_out[...], (((1,), (1,)), ((), ())), preferred_element_type=F32
    )
    power = jnp.mean(updated * updated, axis=1, keepdims=True)
    normed = (updated * lax.rsqrt(power + 1e-6) * gain[...]).astype(BF)
    answer = jnp.dot(normed, w_inc[...], preferred_element_type=F32)
    predicted[...] = answer
    residual = answer - target[...].astype(F32)
    high = residual.astype(BF)
    low = (residual - high.astype(F32)).astype(BF)
    dims = (((0,), (0,)), ((), ()))
    total = lax.dot_general(normed, high, dims, preferred_element_type=F32)
    total = total + lax.dot_general(normed, low, dims, preferred_element_type=F32)
    *grads, cut = grads
    size = grads[0].shape[0]
    for c in range(width // size):
        cut[c] = total[c * size:(c + 1) * size]
    for d, grad in enumerate(grads):
        grad[...] = cut[place[0] ^ d]


def body(
    obs_feat,
    row_valid,
    block_owner,
    block_pattern,
    latent,
    w_query,
    w_key,
    w_value,
    self_bias,
    w_out,
    norm_gain,
    w_inc,
    target,
):
    tiles = lax.axis_size("tile")
    groups = lax.axis_size("head")
    me = lax.axis_index("head")
    blocks = block_owner.shape[0]
    block_rows = obs_feat.shape[0] // blocks
    quarter = block_rows // groups
    cols = obs_feat.shape[1]
    lat_rows, width = latent.shape
    subs = block_pattern.shape[1]
    sub = lat_rows // subs
    local_heads = self_bias.shape[0]
    heads = local_heads * groups
    head_size = width // heads
    share = lat_rows // groups

    def swap(v, axis, mask, size):
        return lax.ppermute(v, axis, [(d, d ^ mask) for d in range(size)])

    whole = lambda *shape: pl.BlockSpec(shape, lambda g, *_: (0,) * len(shape))
    depth = quarter + 8
    alive = jnp.max(block_pattern.T, axis=0)

    def route(spill):
        sent = pl.pallas_call(
            functools.partial(route_kernel, spill),
            grid_spec=pltpu.PrefetchScalarGridSpec(
                num_scalar_prefetch=2,
                grid=(1,),
                in_specs=[
                    whole(blocks, groups, quarter, cols),
                    whole(blocks, block_rows),
                    whole(subs, blocks),
                ],
                out_specs=whole(tiles, groups, depth, cols),
                scratch_shapes=[
                    pltpu.VMEM((groups, blocks + 8, 128), F32),
                    pltpu.SMEM((2 * tiles,), jnp.int32),
                    pltpu.SMEM((blocks + 8,), jnp.int32),
                    pltpu.SMEM((len(NEAR),), jnp.int32),
                ],
            ),
            out_shape=jax.ShapeDtypeStruct((tiles, groups, depth, cols), BF),
            compiler_params=pltpu.CompilerParams(vmem_limit_bytes=32 * 1024 * 1024),
            name="route",
        )(
            block_owner[:, 0],
            alive,
            obs_feat.reshape(blocks, groups, quarter, cols),
            row_valid.reshape(blocks, block_rows),
            block_pattern.T,
        )
        return lax.all_to_all(
            sent.reshape(tiles * groups, depth, cols),
            ("tile", "head"),
            split_axis=0,
            concat_axis=0,
            tiled=True,
        ).reshape(tiles, groups, depth, cols)

    arrived = route(True)
    near = len(NEAR)
    stacked = jnp.concatenate([w_query, w_key, w_value, w_out.T], axis=1)
    nearby = [stacked] + [swap(stacked, "head", d, groups) for d in range(1, groups)]
    turn = jnp.arange(groups, dtype=jnp.int32) ^ me
    biases = [self_bias] + [swap(self_bias, "head", d, groups) for d in range(1, groups)]

    qw, states, numer, wv, wo = pl.pallas_call(
        prepare_kernel,
        grid=(1,),
        in_specs=[pl.BlockSpec(memory_space=pltpu.SMEM)] * groups
        + [whole(width, width)] * groups
        + [whole(lat_rows, width)],
        out_specs=[
            whole(heads, lat_rows, width),
            whole(lat_rows, 128),
            whole(lat_rows, width),
            whole(width, width),
            whole(width, width),
        ],
        out_shape=[
            jax.ShapeDtypeStruct((heads, lat_rows, width), BF),
            jax.ShapeDtypeStruct((lat_rows, 128), F32),
            jax.ShapeDtypeStruct((lat_rows, width), F32),
            jax.ShapeDtypeStruct((width, width), BF),
            jax.ShapeDtypeStruct((width, width), BF),
        ],
        compiler_params=pltpu.CompilerParams(vmem_limit_bytes=32 * 1024 * 1024),
        name="prepare",
    )(*biases, *nearby, latent)

    plan, *held = pl.pallas_call(
        plan_kernel,
        grid=(1,),
        in_specs=[whole(tiles, groups, depth, cols)],
        out_specs=[whole(2 * near, 128)]
        + [whole(n, groups, depth, cols) for n in DEPTHS],
        out_shape=[jax.ShapeDtypeStruct((2 * near, 128), jnp.int32)]
        + [jax.ShapeDtypeStruct((n, groups, depth, cols), BF) for n in DEPTHS],
        scratch_shapes=[
            pltpu.SMEM((2 * near, 128), jnp.int32),
            pltpu.SemaphoreType.DMA,
        ],
        compiler_params=pltpu.CompilerParams(vmem_limit_bytes=32 * 1024 * 1024),
        name="plan",
    )(arrived)
    rest = tiles - sum(DEPTHS)
    starts = [sum(DEPTHS[:m]) for m in range(near)]

    def forward():
        moved = [swap(v, "tile", m, tiles) for m, v in zip(NEAR, held)]
        return *moved, jnp.zeros((rest, groups, depth, cols), BF)

    def again():
        second = route(False)
        parts = [second[a:a + n] for a, n in zip(starts, DEPTHS)]
        return *parts, second[-rest:]

    units = (arrived, *lax.cond(plan[near, 0] > 0, forward, again))
    block = PAIR * sub
    scratch = [
        pltpu.VMEM((SLOTS * tiles, groups, depth, cols), BF),
        pltpu.SemaphoreType.DMA((len(units) + 1,)),
        pltpu.VMEM((subs, 256), jnp.int32),
        pltpu.SMEM((subs, 256), jnp.int32),
        pltpu.VMEM((SLOTS * tiles, 128), F32),
        pltpu.VMEM((groups, share, width + 128), BF),
    ] + [
        shape
        for shape in (
            pltpu.VMEM((CHUNK * quarter, width), BF),
            pltpu.VMEM((heads * sub, width), F32),
            pltpu.VMEM((heads * sub, 128), F32),
            pltpu.VMEM((heads * sub, 128), F32),
        )
        for _ in range(PAIR)
    ]
    partials = pl.pallas_call(
        attend_kernel,
        grid=(subs // PAIR,),
        in_specs=[pl.BlockSpec(memory_space=pl.ANY)] * len(units)
        + [
            pl.BlockSpec((heads, block, width), lambda g: (0, g, 0)),
            pl.BlockSpec((block, 128), lambda g: (g, 0)),
            pl.BlockSpec((block, width), lambda g: (g, 0)),
            whole(width, width),
        ],
        out_specs=[whole(share, width + 128)] * groups,
        scratch_shapes=scratch,
        out_shape=[jax.ShapeDtypeStruct((share, width + 128), BF)] * groups,
        compiler_params=pltpu.CompilerParams(vmem_limit_bytes=48 * 1024 * 1024),
        name="attend",
    )(*units, qw, states, numer, wv)

    received = [partials[0]] + [
        swap(partials[d], "head", d, groups) for d in range(1, groups)
    ]
    row = lambda *shape: pl.BlockSpec(shape, lambda i, m: (m[0], 0))
    mine, *grads = pl.pallas_call(
        finish_kernel,
        grid_spec=pltpu.PrefetchScalarGridSpec(
            num_scalar_prefetch=1,
            grid=(1,),
            in_specs=[whole(share, width + 128)] * groups
            + [
                row(share, width),
                whole(width, width),
                whole(1, width),
                whole(width, 128),
                row(share, 128),
            ],
            out_specs=[whole(share, 128)] + [whole(cols, 128)] * groups,
            scratch_shapes=[pltpu.VMEM((groups, cols, 128), F32)],
        ),
        out_shape=[jax.ShapeDtypeStruct((share, 128), F32)]
        + [jax.ShapeDtypeStruct((cols, 128), F32)] * groups,
        compiler_params=pltpu.CompilerParams(vmem_limit_bytes=32 * 1024 * 1024),
        name="finish",
    )(
        me[None].astype(jnp.int32),
        *received,
        latent,
        wo,
        norm_gain[None, :],
        w_inc,
        target,
    )
    grads = [grads[0]] + [swap(grads[d], "head", d, groups) for d in range(1, groups)]
    grad = (grads[0] + grads[1]) + (grads[2] + grads[3])
    for low, high in ((1, 2), (4, 8), (16, 32)):
        a, b, c = (swap(grad, "tile", m, tiles) for m in (low, high, low + high))
        grad = (grad + a) + (b + c)
    preds = jnp.stack([mine] + [swap(mine, "head", d, groups) for d in range(1, groups)])
    predicted = jnp.take(preds, turn, axis=0).reshape(lat_rows, 128)
    return predicted, grad * (1.0 / math.sqrt(lat_rows * tiles))


def solution(mesh):
    in_specs = (
        P("tile", "head"),
        P("tile"),
        P("tile", None),
        P("tile", None),
        P("tile", None),
        P(None, "head"),
        P(None, "head"),
        P(None, "head"),
        P("head"),
        P("head", None),
        P(),
        P(),
        P("tile", None),
    )
    out_specs = (P("tile", None), P("head", None))
    return jax.shard_map(body, mesh=mesh, in_specs=in_specs, out_specs=out_specs, check_vma=False)
```

profile of v0, /device:TPU:32, one launch (start us, length us, event | category | flops | bytes accessed | tf_op | source)
XLA Modules:
  0.0 188.2 jit_solution(16752214879537712115)
XLA Ops:
  1.3 4.7 %route.3 = bf16[64,4,40,128]{3,2,1,0:T(8,128)(2,1)S(1)} custom-call(s32[64]{0:T(128)} %bitcast.51, s32[64]{0:T(128)S(1)} %reduce_max.9.alive, bf16[64,4,32,128]{3,2,1,0:T(8,128)(2,1)} %bitcast.40, s32[64,128]{1,0:T(8,128)} %bitcast.44, s32[16,64]{1,0:T(8,128)} %bitcast.46), custom_call_target="tpu_custom_call" | custom-call | tf_op jit(solution)/shard_map/route/pallas_call | solution.py:468
  6.1 1.5 copy-done
  7.6 14.4 %all-to-all-start.1 = ((bf16[256,40,128]{2,1,0:T(8,128)(2,1)}), bf16[256,40,128]{2,1,0:T(8,128)(2,1)S(1)}, u32[]{:S(2)}, u32[]{:S(2)}) async-start(bf16[256,40,128]{2,1,0:T(8,128)(2,1)} %bitcast.36), calls=%async_computation.1 | async-start | bytes 5242880 | tf_op jit(solution)/shard_map/all_to_all | solution.py:496
  22.1 1.8 pad_maximum_fusion.refs_4_
  23.9 1.5 collective-permute-start.11
  25.4 2.7 %collective-permute-start.12 = (bf16[512,512]{1,0:T(8,128)(2,1)}, bf16[512,512]{1,0:T(8,128)(2,1)}, u32[]{:S(2)}, u32[]{:S(2)}) collective-permute-start(bf16[512,512]{1,0:T(8,128)(2,1)} %pad_maximum_fusion.refs_4_), channel_id=1, source_target_pairs={{0,2},{1,3},{2,0},{3,1},{4,6},{5,7},{6,4},{7,5},{8,10},{9,11},{10,... | collective-permute-start | bytes 1572872 | tf_op jit(solution)/shard_map/ppermute | solution.py:461
  28.7 2.7 %collective-permute-start.10 = (f32[2]{0:T(128)S(1)}, f32[2]{0:T(128)S(1)}, u32[]{:S(2)}, u32[]{:S(2)}) collective-permute-start(f32[2]{0:T(128)S(1)} %copy-done.12), channel_id=1, source_target_pairs={{0,3},{1,2},{2,1},{3,0},{4,7},{5,6},{6,5},{7,4},{8,11},{9,10},{10,... | collective-permute-start | bytes 32 | tf_op jit(solution)/shard_map/ppermute | solution.py:461
  31.4 40.6 %collective-permute-done.10.refs_3_ = f32[2]{0:T(128)S(1)} collective-permute-done((f32[2]{0:T(128)S(1)}, f32[2]{0:T(128)S(1)}, u32[]{:S(2)}, u32[]{:S(2)}) %collective-permute-start.10) | collective-permute-done | bytes 40 | tf_op jit(solution)/shard_map/ppermute | solution.py:461
  72.1 5.0 %collective-permute-done.9.refs_2_ = f32[2]{0:T(128)S(1)} collective-permute-done((f32[2]{0:T(128)S(1)}, f32[2]{0:T(128)S(1)}, u32[]{:S(2)}, u32[]{:S(2)}) %collective-permute-start.9) | collective-permute-done | bytes 40 | tf_op jit(solution)/shard_map/ppermute | solution.py:461
  77.1 4.6 %prepare.1 = (bf16[8,512,512]{2,1,0:T(8,128)(2,1)S(1)}, f32[512,128]{1,0:T(8,128)S(1)}, f32[512,512]{1,0:T(8,128)S(1)}, bf16[512,512]{1,0:T(8,128)(2,1)S(1)}, bf16[512,512]{1,0:T(8,128)(2,1)S(1)}) custom-call(f32[2]{0:T(128)S(1)} %copy-done.12, f32[2]{0:T(128)S(1)} %collective-permute-done.8.refs_1_, f32[2]{0:T(128)S(1)} %collective-permute-done.9.refs_2_, ...), custom_call_target="tpu_custom_call" | custom-call | tf_op jit(solution)/shard_map/prepare/pallas_call | solution.py:511
  81.8 2.0 %copy-done.1 = bf16[8,512,512]{2,1,0:T(8,128)(2,1)} copy-done((bf16[8,512,512]{2,1,0:T(8,128)(2,1)}, bf16[8,512,512]{2,1,0:T(8,128)(2,1)S(1)}, u32[]{:S(2)}) %copy-start.1) | copy-done | bytes 4194328
  83.7 1.1 copy-done.3
  84.8 0.9 copy-done.5
  86.5 1.2 all-to-all-done.1
  87.7 1.8 plan.1
  90.7 26.8 %conditional.1 = (bf16[6,4,40,128]{3,2,1,0:T(8,128)(2,1)}, bf16[6,4,40,128]{3,2,1,0:T(8,128)(2,1)}, bf16[6,4,40,128]{3,2,1,0:T(8,128)(2,1)}, bf16[6,4,40,128]{3,...) conditional(s32[]{:T(128)} %bitcast.22, ...), branch_computations={%region_1.0_spmd, %region_2.0_spmd} | conditional | bytes 10485832 | solution.py:562
  91.3 2.8 %collective-permute-start.7 = (bf16[2,4,40,128]{3,2,1,0:T(8,128)(2,1)S(1)}, bf16[2,4,40,128]{3,2,1,0:T(8,128)(2,1)}, u32[]{:S(2)}, u32[]{:S(2)}) collective-permute-start(bf16[2,4,40,128]{3,2,1,0:T(8,128)(2,1)S(1)} %get-tuple-element.38), channel_id=1, source_target_pairs={{0,128},{4,132},{8,136},{12,140},{16,144},{20,148},{24,152},{28,15... | collective-permute-start | bytes 245768 | tf_op jit(solution)/shard_map/cond/branch_1_fun/ppermute | solution.py:461
  94.0 1.6 collective-permute-start.3
  95.6 7.0 %collective-permute-done.7 = bf16[2,4,40,128]{3,2,1,0:T(8,128)(2,1)} collective-permute-done((bf16[2,4,40,128]{3,2,1,0:T(8,128)(2,1)S(1)}, bf16[2,4,40,128]{3,2,1,0:T(8,128)(2,1)}, u32[]{:S(2)}, u32[]{:S(2)}) %collective-permute-start.7) | collective-permute-done | bytes 81952 | tf_op jit(solution)/shard_map/cond/branch_1_fun/ppermute | solution.py:461
  103.0 1.2 collective-permute-start.5
  104.2 1.5 collective-permute-start.6
  105.8 5.7 %collective-permute-done.4 = bf16[6,4,40,128]{3,2,1,0:T(8,128)(2,1)} collective-permute-done((bf16[6,4,40,128]{3,2,1,0:T(8,128)(2,1)S(1)}, bf16[6,4,40,128]{3,2,1,0:T(8,128)(2,1)}, u32[]{:S(2)}, u32[]{:S(2)}) %collective-permute-start.4) | collective-permute-done | bytes 245792 | tf_op jit(solution)/shard_map/cond/branch_1_fun/ppermute | solution.py:461
  111.6 5.6 %collective-permute-done.6 = bf16[6,4,40,128]{3,2,1,0:T(8,128)(2,1)} collective-permute-done((bf16[6,4,40,128]{3,2,1,0:T(8,128)(2,1)S(1)}, bf16[6,4,40,128]{3,2,1,0:T(8,128)(2,1)}, u32[]{:S(2)}, u32[]{:S(2)}) %collective-permute-start.6) | collective-permute-done | bytes 245792 | tf_op jit(solution)/shard_map/cond/branch_1_fun/ppermute | solution.py:461
  117.5 0.9 copy-done.14
  118.4 1.2 copy-done.4
  119.7 1.0 copy-done.8
  120.7 13.5 %attend.1 = (bf16[128,640]{1,0:T(8,128)(2,1)S(1)}, bf16[128,640]{1,0:T(8,128)(2,1)S(1)}, bf16[128,640]{1,0:T(8,128)(2,1)S(1)}, bf16[128,640]{1,0:T(8,128)(2,1)S(1)}) custom-call(bf16[64,4,40,128]{3,2,1,0:T(8,128)(2,1)S(1)} %bitcast.35, bf16[6,4,40,128]{3,2,1,0:T(8,128)(2,1)} %get-tuple-element.82.refs_1_, bf16[6,4,40,128]{3,2,1,0:T(8,128)(2,1)} %get-tuple-element.83.refs_2_, ...), custom_call_target="tpu_custom_call" | custom-call | tf_op jit(solution)/shard_map/attend/pallas_call | solution.py:581
  134.9 1.4 collective-permute-start.15
  136.3 2.7 %collective-permute-start.16 = (bf16[128,640]{1,0:T(8,128)(2,1)S(1)}, bf16[128,640]{1,0:T(8,128)(2,1)S(1)}, u32[]{:S(2)}, u32[]{:S(2)}) collective-permute-start(bf16[128,640]{1,0:T(8,128)(2,1)S(1)} %get-tuple-element.98), channel_id=1, source_target_pairs={{0,3},{1,2},{2,1},{3,0},{4,7},{5,6},{6,5},{7,4},{8,11},{9,10},{10,... | collective-permute-start | bytes 491528 | tf_op jit(solution)/shard_map/ppermute | solution.py:461
  139.0 2.3 %collective-permute-done.14.r1 = bf16[128,640]{1,0:T(8,128)(2,1)S(1)} collective-permute-done((bf16[128,640]{1,0:T(8,128)(2,1)S(1)}, bf16[128,640]{1,0:T(8,128)(2,1)S(1)}, u32[]{:S(2)}, u32[]{:S(2)}) %collective-permute-start.14) | collective-permute-done | bytes 163872 | tf_op jit(solution)/shard_map/ppermute | solution.py:461
  141.4 2.4 %collective-permute-done.15.r2 = bf16[128,640]{1,0:T(8,128)(2,1)S(1)} collective-permute-done((bf16[128,640]{1,0:T(8,128)(2,1)S(1)}, bf16[128,640]{1,0:T(8,128)(2,1)S(1)}, u32[]{:S(2)}, u32[]{:S(2)}) %collective-permute-start.15) | collective-permute-done | bytes 163872 | tf_op jit(solution)/shard_map/ppermute | solution.py:461
  143.8 2.4 %collective-permute-done.16.r3 = bf16[128,640]{1,0:T(8,128)(2,1)S(1)} collective-permute-done((bf16[128,640]{1,0:T(8,128)(2,1)S(1)}, bf16[128,640]{1,0:T(8,128)(2,1)S(1)}, u32[]{:S(2)}, u32[]{:S(2)}) %collective-permute-start.16) | collective-permute-done | bytes 163872 | tf_op jit(solution)/shard_map/ppermute | solution.py:461
  146.2 1.4 finish.1
  147.7 4.1 %collective-permute-start.21 = (f32[128,128]{1,0:T(8,128)S(1)}, f32[128,128]{1,0:T(8,128)S(1)}, u32[]{:S(2)}, u32[]{:S(2)}) collective-permute-start(f32[128,128]{1,0:T(8,128)S(1)} %get-tuple-element.103), channel_id=1, source_target_pairs={{0,2},{1,3},{2,0},{3,1},{4,6},{5,7},{6,4},{7,5},{8,10},{9,11},{10,... | collective-permute-start | bytes 196616 | tf_op jit(solution)/shard_map/ppermute | solution.py:461
  152.5 2.3 %collective-permute-done.21 = f32[128,128]{1,0:T(8,128)S(1)} collective-permute-done((f32[128,128]{1,0:T(8,128)S(1)}, f32[128,128]{1,0:T(8,128)S(1)}, u32[]{:S(2)}, u32[]{:S(2)}) %collective-permute-start.21) | collective-permute-done | bytes 65568 | tf_op jit(solution)/shard_map/ppermute | solution.py:461
  154.9 2.5 %collective-permute-done.22 = f32[128,128]{1,0:T(8,128)S(1)} collective-permute-done((f32[128,128]{1,0:T(8,128)S(1)}, f32[128,128]{1,0:T(8,128)S(1)}, u32[]{:S(2)}, u32[]{:S(2)}) %collective-permute-start.22) | collective-permute-done | bytes 65568 | tf_op jit(solution)/shard_map/ppermute | solution.py:461
  157.7 1.3 collective-permute-start.24
  159.6 2.0 %collective-permute-start.18 = (f32[128,128]{1,0:T(8,128)S(1)}, f32[128,128]{1,0:T(8,128)S(1)}, u32[]{:S(2)}, u32[]{:S(2)}) collective-permute-start(f32[128,128]{1,0:T(8,128)S(1)} %get-tuple-element.100), channel_id=1, source_target_pairs={{0,2},{1,3},{2,0},{3,1},{4,6},{5,7},{6,4},{7,5},{8,10},{9,11},{10,... | collective-permute-start | bytes 196616 | tf_op jit(solution)/shard_map/ppermute | solution.py:461
  161.6 2.7 %collective-permute-start.19 = (f32[128,128]{1,0:T(8,128)S(1)}, f32[128,128]{1,0:T(8,128)S(1)}, u32[]{:S(2)}, u32[]{:S(2)}) collective-permute-start(f32[128,128]{1,0:T(8,128)S(1)} %get-tuple-element.100), channel_id=1, source_target_pairs={{0,3},{1,2},{2,1},{3,0},{4,7},{5,6},{6,5},{7,4},{8,11},{9,10},{10,... | collective-permute-start | bytes 196616 | tf_op jit(solution)/shard_map/ppermute | solution.py:461
  164.3 3.4 %collective-permute-start.26 = (f32[128,128]{1,0:T(8,128)S(1)}, f32[128,128]{1,0:T(8,128)S(1)}, u32[]{:S(2)}, u32[]{:S(2)}) collective-permute-start(f32[128,128]{1,0:T(8,128)S(1)} %add_add_fusion.1), channel_id=1, source_target_pairs={{0,16},{4,20},{8,24},{12,28},{16,0},{20,4},{24,8},{28,12},{32,48},... | collective-permute-start | bytes 196616 | tf_op jit(solution)/shard_map/ppermute | solution.py:461
  167.7 3.1 %collective-permute-start.27 = (f32[128,128]{1,0:T(8,128)S(1)}, f32[128,128]{1,0:T(8,128)S(1)}, u32[]{:S(2)}, u32[]{:S(2)}) collective-permute-start(f32[128,128]{1,0:T(8,128)S(1)} %add_add_fusion.1), channel_id=1, source_target_pairs={{0,32},{4,36},{8,40},{12,44},{16,48},{20,52},{24,56},{28,60},{32,0... | collective-permute-start | bytes 196616 | tf_op jit(solution)/shard_map/ppermute | solution.py:461
  172.0 5.3 %collective-permute-done.27 = f32[128,128]{1,0:T(8,128)S(1)} collective-permute-done((f32[128,128]{1,0:T(8,128)S(1)}, f32[128,128]{1,0:T(8,128)S(1)}, u32[]{:S(2)}, u32[]{:S(2)}) %collective-permute-start.27) | collective-permute-done | bytes 65568 | tf_op jit(solution)/shard_map/ppermute | solution.py:461
  177.3 1.0 collective-permute-done.28
  178.4 3.7 %collective-permute-start.30 = (f32[128,128]{1,0:T(8,128)S(1)}, f32[128,128]{1,0:T(8,128)S(1)}, u32[]{:S(2)}, u32[]{:S(2)}) collective-permute-start(f32[128,128]{1,0:T(8,128)S(1)} %add_add_fusion), channel_id=1, source_target_pairs={{0,128},{4,132},{8,136},{12,140},{16,144},{20,148},{24,152},{28,15... | collective-permute-start | bytes 196616 | tf_op jit(solution)/shard_map/ppermute | solution.py:461
  182.1 1.0 collective-permute-start.31
  183.1 0.8 bitcast_select_fusion
  184.0 1.5 collective-permute-done.30
  185.5 2.1 %collective-permute-done.31 = f32[128,128]{1,0:T(8,128)S(1)} collective-permute-done((f32[128,128]{1,0:T(8,128)S(1)}, f32[128,128]{1,0:T(8,128)S(1)}, u32[]{:S(2)}, u32[]{:S(2)}) %collective-permute-start.31) | collective-permute-done | bytes 65568 | tf_op jit(solution)/shard_map/ppermute | solution.py:461
  (80 shorter events, 8.4 us)
Async XLA Ops:
  6.0 1.5 copy-start
  7.6 14.4 %copy-start.16 = (bf16[128,512]{1,0:T(8,128)(2,1)S(1)}, bf16[128,512]{1,0:T(8,128)(2,1)}, u32[]{:S(2)}) copy-start(bf16[128,512]{1,0:T(8,128)(2,1)} %param.24) | copy-start | bytes 393220
  7.6 14.5 %copy-start.17 = (bf16[512,128]{1,0:T(8,128)(2,1)S(1)}, bf16[512,128]{1,0:T(8,128)(2,1)}, u32[]{:S(2)}) copy-start(bf16[512,128]{1,0:T(8,128)(2,1)} %param.22) | copy-start | bytes 393220
  7.6 21.1 %copy-start.12 = (f32[2]{0:T(128)S(1)}, f32[2]{0:T(128)}, u32[]{:S(2)}) copy-start(f32[2]{0:T(128)} %refs_0_.1) | copy-start | bytes 28
  7.6 69.6 %copy-start.2 = (bf16[512,512]{1,0:T(8,128)(2,1)S(1)}, bf16[512,512]{1,0:T(8,128)(2,1)}, u32[]{:S(2)}) copy-start(bf16[512,512]{1,0:T(8,128)(2,1)} %lat.1) | copy-start | bytes 1572868
  7.6 80.1 %all-to-all-start.1 = ((bf16[256,40,128]{2,1,0:T(8,128)(2,1)}), bf16[256,40,128]{2,1,0:T(8,128)(2,1)S(1)}, u32[]{:S(2)}, u32[]{:S(2)}) async-start(bf16[256,40,128]{2,1,0:T(8,128)(2,1)} %bitcast.36), calls=%async_computation.1 | async-start | bytes 5242880 | tf_op jit(solution)/shard_map/all_to_all | solution.py:496
  23.9 53.2 %collective-permute-start.11 = (bf16[512,512]{1,0:T(8,128)(2,1)}, bf16[512,512]{1,0:T(8,128)(2,1)}, u32[]{:S(2)}, u32[]{:S(2)}) collective-permute-start(bf16[512,512]{1,0:T(8,128)(2,1)} %pad_maximum_fusion.refs_4_), channel_id=1, source_target_pairs={{0,1},{1,0},{2,3},{3,2},{4,5},{5,4},{6,7},{7,6},{8,9},{9,8},{10,11... | collective-permute-start | bytes 1572872 | tf_op jit(solution)/shard_map/ppermute | solution.py:461
  25.4 51.7 %collective-permute-start.12 = (bf16[512,512]{1,0:T(8,128)(2,1)}, bf16[512,512]{1,0:T(8,128)(2,1)}, u32[]{:S(2)}, u32[]{:S(2)}) collective-permute-start(bf16[512,512]{1,0:T(8,128)(2,1)} %pad_maximum_fusion.refs_4_), channel_id=1, source_target_pairs={{0,2},{1,3},{2,0},{3,1},{4,6},{5,7},{6,4},{7,5},{8,10},{9,11},{10,... | collective-permute-start | bytes 1572872 | tf_op jit(solution)/shard_map/ppermute | solution.py:461
  28.1 49.0 %collective-permute-start.13 = (bf16[512,512]{1,0:T(8,128)(2,1)}, bf16[512,512]{1,0:T(8,128)(2,1)}, u32[]{:S(2)}, u32[]{:S(2)}) collective-permute-start(bf16[512,512]{1,0:T(8,128)(2,1)} %pad_maximum_fusion.refs_4_), channel_id=1, source_target_pairs={{0,3},{1,2},{2,1},{3,0},{4,7},{5,6},{6,5},{7,4},{8,11},{9,10},{10,... | collective-permute-start | bytes 1572872 | tf_op jit(solution)/shard_map/ppermute | solution.py:461
  28.7 43.4 %collective-permute-start.10 = (f32[2]{0:T(128)S(1)}, f32[2]{0:T(128)S(1)}, u32[]{:S(2)}, u32[]{:S(2)}) collective-permute-start(f32[2]{0:T(128)S(1)} %copy-done.12), channel_id=1, source_target_pairs={{0,3},{1,2},{2,1},{3,0},{4,7},{5,6},{6,5},{7,4},{8,11},{9,10},{10,... | collective-permute-start | bytes 32 | tf_op jit(solution)/shard_map/ppermute | solution.py:461
  31.4 40.7 %collective-permute-start.8 = (f32[2]{0:T(128)S(1)}, f32[2]{0:T(128)S(1)}, u32[]{:S(2)}, u32[]{:S(2)}) collective-permute-start(f32[2]{0:T(128)S(1)} %copy-done.12), channel_id=1, source_target_pairs={{0,1},{1,0},{2,3},{3,2},{4,5},{5,4},{6,7},{7,6},{8,9},{9,8},{10,11... | collective-permute-start | bytes 32 | tf_op jit(solution)/shard_map/ppermute | solution.py:461
  31.4 59.3 %copy-start.15 = (s32[8192]{0:T(1024)S(1)}, s32[8192]{0:T(1024)}, u32[]{:S(2)}) copy-start(s32[8192]{0:T(1024)} %param.16) | copy-start | bytes 98308
  31.4 59.3 %copy-start.18 = (s32[64,16]{0,1:T(8,128)S(1)}, s32[64,16]{0,1:T(8,128)}, u32[]{:S(2)}) copy-start(s32[64,16]{0,1:T(8,128)} %param.18) | copy-start | bytes 12292
  31.4 59.3 %copy-start.19 = (s32[64,1]{0,1:T(1,128)S(1)}, s32[64,1]{0,1:T(1,128)}, u32[]{:S(2)}) copy-start(s32[64,1]{0,1:T(1,128)} %param.17) | copy-start | bytes 772
  72.1 5.1 %collective-permute-start.9 = (f32[2]{0:T(128)S(1)}, f32[2]{0:T(128)S(1)}, u32[]{:S(2)}, u32[]{:S(2)}) collective-permute-start(f32[2]{0:T(128)S(1)} %copy-done.12), channel_id=1, source_target_pairs={{0,2},{1,3},{2,0},{3,1},{4,6},{5,7},{6,4},{7,5},{8,10},{9,11},{10,... | collective-permute-start | bytes 32 | tf_op jit(solution)/shard_map/ppermute | solution.py:461
  81.7 2.0 %copy-start.1 = (bf16[8,512,512]{2,1,0:T(8,128)(2,1)}, bf16[8,512,512]{2,1,0:T(8,128)(2,1)S(1)}, u32[]{:S(2)}) copy-start(bf16[8,512,512]{2,1,0:T(8,128)(2,1)S(1)} %get-tuple-element.91.refs_10_) | copy-start | bytes 12582916
  87.6 3.0 %copy-start.13 = (bf16[8192,128]{1,0:T(8,128)(2,1)S(1)}, bf16[8192,128]{1,0:T(8,128)(2,1)}, u32[]{:S(2)}) copy-start(bf16[8192,128]{1,0:T(8,128)(2,1)} %param.15) | copy-start | bytes 6291460
  90.7 12.3 %collective-permute-start = (bf16[6,4,40,128]{3,2,1,0:T(8,128)(2,1)S(1)}, bf16[6,4,40,128]{3,2,1,0:T(8,128)(2,1)}, u32[]{:S(2)}, u32[]{:S(2)}) collective-permute-start(bf16[6,4,40,128]{3,2,1,0:T(8,128)(2,1)S(1)} %get-tuple-element.31), channel_id=1, source_target_pairs={{0,4},{4,0},{8,12},{12,8},{16,20},{20,16},{24,28},{28,24},{32,36},... | collective-permute-start | bytes 737288 | tf_op jit(solution)/shard_map/cond/branch_1_fun/ppermute | solution.py:461
  90.8 13.4 %collective-permute-start.1 = (bf16[6,4,40,128]{3,2,1,0:T(8,128)(2,1)S(1)}, bf16[6,4,40,128]{3,2,1,0:T(8,128)(2,1)}, u32[]{:S(2)}, u32[]{:S(2)}) collective-permute-start(bf16[6,4,40,128]{3,2,1,0:T(8,128)(2,1)S(1)} %get-tuple-element.32), channel_id=1, source_target_pairs={{0,64},{4,68},{8,72},{12,76},{16,80},{20,84},{24,88},{28,92},{32,9... | collective-permute-start | bytes 737288 | tf_op jit(solution)/shard_map/cond/branch_1_fun/ppermute | solution.py:461
  91.3 11.4 %collective-permute-start.7 = (bf16[2,4,40,128]{3,2,1,0:T(8,128)(2,1)S(1)}, bf16[2,4,40,128]{3,2,1,0:T(8,128)(2,1)}, u32[]{:S(2)}, u32[]{:S(2)}) collective-permute-start(bf16[2,4,40,128]{3,2,1,0:T(8,128)(2,1)S(1)} %get-tuple-element.38), channel_id=1, source_target_pairs={{0,128},{4,132},{8,136},{12,140},{16,144},{20,148},{24,152},{28,15... | collective-permute-start | bytes 245768 | tf_op jit(solution)/shard_map/cond/branch_1_fun/ppermute | solution.py:461
  94.0 11.8 %collective-permute-start.2 = (bf16[6,4,40,128]{3,2,1,0:T(8,128)(2,1)S(1)}, bf16[6,4,40,128]{3,2,1,0:T(8,128)(2,1)}, u32[]{:S(2)}, u32[]{:S(2)}) collective-permute-start(bf16[6,4,40,128]{3,2,1,0:T(8,128)(2,1)S(1)} %get-tuple-element.33), channel_id=1, source_target_pairs={{0,68},{4,64},{8,76},{12,72},{16,84},{20,80},{24,92},{28,88},{32,1... | collective-permute-start | bytes 737288 | tf_op jit(solution)/shard_map/cond/branch_1_fun/ppermute | solution.py:461
  94.0 11.8 %collective-permute-start.3 = (bf16[6,4,40,128]{3,2,1,0:T(8,128)(2,1)S(1)}, bf16[6,4,40,128]{3,2,1,0:T(8,128)(2,1)}, u32[]{:S(2)}, u32[]{:S(2)}) collective-permute-start(bf16[6,4,40,128]{3,2,1,0:T(8,128)(2,1)S(1)} %get-tuple-element.34), channel_id=1, source_target_pairs={{0,192},{4,196},{8,200},{12,204},{16,208},{20,212},{24,216},{28,22... | collective-permute-start | bytes 737288 | tf_op jit(solution)/shard_map/cond/branch_1_fun/ppermute | solution.py:461
  102.6 8.9 %collective-permute-start.4 = (bf16[6,4,40,128]{3,2,1,0:T(8,128)(2,1)S(1)}, bf16[6,4,40,128]{3,2,1,0:T(8,128)(2,1)}, u32[]{:S(2)}, u32[]{:S(2)}) collective-permute-start(bf16[6,4,40,128]{3,2,1,0:T(8,128)(2,1)S(1)} %get-tuple-element.35), channel_id=1, source_target_pairs={{0,196},{4,192},{8,204},{12,200},{16,212},{20,208},{24,220},{28,21... | collective-permute-start | bytes 737288 | tf_op jit(solution)/shard_map/cond/branch_1_fun/ppermute | solution.py:461
  103.0 8.6 %collective-permute-start.5 = (bf16[6,4,40,128]{3,2,1,0:T(8,128)(2,1)S(1)}, bf16[6,4,40,128]{3,2,1,0:T(8,128)(2,1)}, u32[]{:S(2)}, u32[]{:S(2)}) collective-permute-start(bf16[6,4,40,128]{3,2,1,0:T(8,128)(2,1)S(1)} %get-tuple-element.36), channel_id=1, source_target_pairs={{0,8},{4,12},{8,0},{12,4},{16,24},{20,28},{24,16},{28,20},{32,40},... | collective-permute-start | bytes 737288 | tf_op jit(solution)/shard_map/cond/branch_1_fun/ppermute | solution.py:461
  104.2 13.0 %collective-permute-start.6 = (bf16[6,4,40,128]{3,2,1,0:T(8,128)(2,1)S(1)}, bf16[6,4,40,128]{3,2,1,0:T(8,128)(2,1)}, u32[]{:S(2)}, u32[]{:S(2)}) collective-permute-start(bf16[6,4,40,128]{3,2,1,0:T(8,128)(2,1)S(1)} %get-tuple-element.37), channel_id=1, source_target_pairs={{0,12},{4,8},{8,4},{12,0},{16,28},{20,24},{24,20},{28,16},{32,44},... | collective-permute-start | bytes 737288 | tf_op jit(solution)/shard_map/cond/branch_1_fun/ppermute | solution.py:461
  118.4 1.2 copy-start.4
  120.7 25.5 %copy-start.6 = (bf16[512,512]{1,0:T(8,128)(2,1)S(1)}, bf16[512,512]{1,0:T(8,128)(2,1)}, u32[]{:S(2)}) copy-start(bf16[512,512]{1,0:T(8,128)(2,1)} %copy-done.5) | copy-start | bytes 1572868
  120.7 25.5 %copy-start.9 = (bf16[512,128]{1,0:T(8,128)(2,1)S(1)}, bf16[512,128]{1,0:T(8,128)(2,1)}, u32[]{:S(2)}) copy-start(bf16[512,128]{1,0:T(8,128)(2,1)} %w_inc.1) | copy-start | bytes 393220
  120.7 25.5 %copy-start.10 = (bf16[512,128]{1,0:T(8,128)(2,1)S(1)}, bf16[512,128]{1,0:T(8,128)(2,1)}, u32[]{:S(2)}) copy-start(bf16[512,128]{1,0:T(8,128)(2,1)} %target.1) | copy-start | bytes 393220
  120.7 25.5 %copy-start.11 = (f32[512]{0:T(512)S(1)}, f32[512]{0:T(512)}, u32[]{:S(2)}) copy-start(f32[512]{0:T(512)} %param.25) | copy-start | bytes 6148
  134.2 7.2 %collective-permute-start.14 = (bf16[128,640]{1,0:T(8,128)(2,1)S(1)}, bf16[128,640]{1,0:T(8,128)(2,1)S(1)}, u32[]{:S(2)}, u32[]{:S(2)}) collective-permute-start(bf16[128,640]{1,0:T(8,128)(2,1)S(1)} %get-tuple-element.96), channel_id=1, source_target_pairs={{0,1},{1,0},{2,3},{3,2},{4,5},{5,4},{6,7},{7,6},{8,9},{9,8},{10,11... | collective-permute-start | bytes 491528 | tf_op jit(solution)/shard_map/ppermute | solution.py:461
  134.9 9.0 %collective-permute-start.15 = (bf16[128,640]{1,0:T(8,128)(2,1)S(1)}, bf16[128,640]{1,0:T(8,128)(2,1)S(1)}, u32[]{:S(2)}, u32[]{:S(2)}) collective-permute-start(bf16[128,640]{1,0:T(8,128)(2,1)S(1)} %get-tuple-element.97), channel_id=1, source_target_pairs={{0,2},{1,3},{2,0},{3,1},{4,6},{5,7},{6,4},{7,5},{8,10},{9,11},{10,... | collective-permute-start | bytes 491528 | tf_op jit(solution)/shard_map/ppermute | solution.py:461
  136.3 9.9 %collective-permute-start.16 = (bf16[128,640]{1,0:T(8,128)(2,1)S(1)}, bf16[128,640]{1,0:T(8,128)(2,1)S(1)}, u32[]{:S(2)}, u32[]{:S(2)}) collective-permute-start(bf16[128,640]{1,0:T(8,128)(2,1)S(1)} %get-tuple-element.98), channel_id=1, source_target_pairs={{0,3},{1,2},{2,1},{3,0},{4,7},{5,6},{6,5},{7,4},{8,11},{9,10},{10,... | collective-permute-start | bytes 491528 | tf_op jit(solution)/shard_map/ppermute | solution.py:461
  147.6 4.9 %collective-permute-start.20 = (f32[128,128]{1,0:T(8,128)S(1)}, f32[128,128]{1,0:T(8,128)S(1)}, u32[]{:S(2)}, u32[]{:S(2)}) collective-permute-start(f32[128,128]{1,0:T(8,128)S(1)} %get-tuple-element.102), channel_id=1, source_target_pairs={{0,1},{1,0},{2,3},{3,2},{4,5},{5,4},{6,7},{7,6},{8,9},{9,8},{10,11... | collective-permute-start | bytes 196616 | tf_op jit(solution)/shard_map/ppermute | solution.py:461
  147.7 7.1 %collective-permute-start.21 = (f32[128,128]{1,0:T(8,128)S(1)}, f32[128,128]{1,0:T(8,128)S(1)}, u32[]{:S(2)}, u32[]{:S(2)}) collective-permute-start(f32[128,128]{1,0:T(8,128)S(1)} %get-tuple-element.103), channel_id=1, source_target_pairs={{0,2},{1,3},{2,0},{3,1},{4,6},{5,7},{6,4},{7,5},{8,10},{9,11},{10,... | collective-permute-start | bytes 196616 | tf_op jit(solution)/shard_map/ppermute | solution.py:461
  151.9 5.5 %collective-permute-start.22 = (f32[128,128]{1,0:T(8,128)S(1)}, f32[128,128]{1,0:T(8,128)S(1)}, u32[]{:S(2)}, u32[]{:S(2)}) collective-permute-start(f32[128,128]{1,0:T(8,128)S(1)} %get-tuple-element.104), channel_id=1, source_target_pairs={{0,3},{1,2},{2,1},{3,0},{4,7},{5,6},{6,5},{7,4},{8,11},{9,10},{10,... | collective-permute-start | bytes 196616 | tf_op jit(solution)/shard_map/ppermute | solution.py:461
  157.4 4.3 %collective-permute-start.23 = (f32[128,128]{1,0:T(8,128)S(1)}, f32[128,128]{1,0:T(8,128)S(1)}, u32[]{:S(2)}, u32[]{:S(2)}) collective-permute-start(f32[128,128]{1,0:T(8,128)S(1)} %add_add_fusion.2), channel_id=1, source_target_pairs={{0,4},{4,0},{8,12},{12,8},{16,20},{20,16},{24,28},{28,24},{32,36},... | collective-permute-start | bytes 196616 | tf_op jit(solution)/shard_map/ppermute | solution.py:461
  157.7 6.6 %collective-permute-start.24 = (f32[128,128]{1,0:T(8,128)S(1)}, f32[128,128]{1,0:T(8,128)S(1)}, u32[]{:S(2)}, u32[]{:S(2)}) collective-permute-start(f32[128,128]{1,0:T(8,128)S(1)} %add_add_fusion.2), channel_id=1, source_target_pairs={{0,8},{4,12},{8,0},{12,4},{16,24},{20,28},{24,16},{28,20},{32,40},... | collective-permute-start | bytes 196616 | tf_op jit(solution)/shard_map/ppermute | solution.py:461
  159.0 5.3 %collective-permute-start.25 = (f32[128,128]{1,0:T(8,128)S(1)}, f32[128,128]{1,0:T(8,128)S(1)}, u32[]{:S(2)}, u32[]{:S(2)}) collective-permute-start(f32[128,128]{1,0:T(8,128)S(1)} %add_add_fusion.2), channel_id=1, source_target_pairs={{0,12},{4,8},{8,4},{12,0},{16,28},{20,24},{24,20},{28,16},{32,44},... | collective-permute-start | bytes 196616 | tf_op jit(solution)/shard_map/ppermute | solution.py:461
  159.6 11.2 %collective-permute-start.17 = (f32[128,128]{1,0:T(8,128)S(1)}, f32[128,128]{1,0:T(8,128)S(1)}, u32[]{:S(2)}, u32[]{:S(2)}) collective-permute-start(f32[128,128]{1,0:T(8,128)S(1)} %get-tuple-element.100), channel_id=1, source_target_pairs={{0,1},{1,0},{2,3},{3,2},{4,5},{5,4},{6,7},{7,6},{8,9},{9,8},{10,11... | collective-permute-start | bytes 196616 | tf_op jit(solution)/shard_map/ppermute | solution.py:461
  159.6 11.8 %collective-permute-start.18 = (f32[128,128]{1,0:T(8,128)S(1)}, f32[128,128]{1,0:T(8,128)S(1)}, u32[]{:S(2)}, u32[]{:S(2)}) collective-permute-start(f32[128,128]{1,0:T(8,128)S(1)} %get-tuple-element.100), channel_id=1, source_target_pairs={{0,2},{1,3},{2,0},{3,1},{4,6},{5,7},{6,4},{7,5},{8,10},{9,11},{10,... | collective-permute-start | bytes 196616 | tf_op jit(solution)/shard_map/ppermute | solution.py:461
  161.6 9.7 %collective-permute-start.19 = (f32[128,128]{1,0:T(8,128)S(1)}, f32[128,128]{1,0:T(8,128)S(1)}, u32[]{:S(2)}, u32[]{:S(2)}) collective-permute-start(f32[128,128]{1,0:T(8,128)S(1)} %get-tuple-element.100), channel_id=1, source_target_pairs={{0,3},{1,2},{2,1},{3,0},{4,7},{5,6},{6,5},{7,4},{8,11},{9,10},{10,... | collective-permute-start | bytes 196616 | tf_op jit(solution)/shard_map/ppermute | solution.py:461
  164.3 7.6 %collective-permute-start.26 = (f32[128,128]{1,0:T(8,128)S(1)}, f32[128,128]{1,0:T(8,128)S(1)}, u32[]{:S(2)}, u32[]{:S(2)}) collective-permute-start(f32[128,128]{1,0:T(8,128)S(1)} %add_add_fusion.1), channel_id=1, source_target_pairs={{0,16},{4,20},{8,24},{12,28},{16,0},{20,4},{24,8},{28,12},{32,48},... | collective-permute-start | bytes 196616 | tf_op jit(solution)/shard_map/ppermute | solution.py:461
  167.7 9.6 %collective-permute-start.27 = (f32[128,128]{1,0:T(8,128)S(1)}, f32[128,128]{1,0:T(8,128)S(1)}, u32[]{:S(2)}, u32[]{:S(2)}) collective-permute-start(f32[128,128]{1,0:T(8,128)S(1)} %add_add_fusion.1), channel_id=1, source_target_pairs={{0,32},{4,36},{8,40},{12,44},{16,48},{20,52},{24,56},{28,60},{32,0... | collective-permute-start | bytes 196616 | tf_op jit(solution)/shard_map/ppermute | solution.py:461
  170.8 7.5 %collective-permute-start.28 = (f32[128,128]{1,0:T(8,128)S(1)}, f32[128,128]{1,0:T(8,128)S(1)}, u32[]{:S(2)}, u32[]{:S(2)}) collective-permute-start(f32[128,128]{1,0:T(8,128)S(1)} %add_add_fusion.1), channel_id=1, source_target_pairs={{0,48},{4,52},{8,56},{12,60},{16,32},{20,36},{24,40},{28,44},{32,1... | collective-permute-start | bytes 196616 | tf_op jit(solution)/shard_map/ppermute | solution.py:461
  178.3 5.6 %collective-permute-start.29 = (f32[128,128]{1,0:T(8,128)S(1)}, f32[128,128]{1,0:T(8,128)S(1)}, u32[]{:S(2)}, u32[]{:S(2)}) collective-permute-start(f32[128,128]{1,0:T(8,128)S(1)} %add_add_fusion), channel_id=1, source_target_pairs={{0,64},{4,68},{8,72},{12,76},{16,80},{20,84},{24,88},{28,92},{32,9... | collective-permute-start | bytes 196616 | tf_op jit(solution)/shard_map/ppermute | solution.py:461
  178.4 7.0 %collective-permute-start.30 = (f32[128,128]{1,0:T(8,128)S(1)}, f32[128,128]{1,0:T(8,128)S(1)}, u32[]{:S(2)}, u32[]{:S(2)}) collective-permute-start(f32[128,128]{1,0:T(8,128)S(1)} %add_add_fusion), channel_id=1, source_target_pairs={{0,128},{4,132},{8,136},{12,140},{16,144},{20,148},{24,152},{28,15... | collective-permute-start | bytes 196616 | tf_op jit(solution)/shard_map/ppermute | solution.py:461
  182.1 5.5 %collective-permute-start.31 = (f32[128,128]{1,0:T(8,128)S(1)}, f32[128,128]{1,0:T(8,128)S(1)}, u32[]{:S(2)}, u32[]{:S(2)}) collective-permute-start(f32[128,128]{1,0:T(8,128)S(1)} %add_add_fusion), channel_id=1, source_target_pairs={{0,192},{4,196},{8,200},{12,204},{16,208},{20,212},{24,216},{28,22... | collective-permute-start | bytes 196616 | tf_op jit(solution)/shard_map/ppermute | solution.py:461
  (5 other events, 4.7 us)
where the time goes:
time: 189 us; the launch traced here: 188 us
  waiting for transfers between devices  87.4 us (46%)
  starting transfers between devices  58 us (31%)
  Pallas kernels  26 us (14%)
  local copies, waits for them, and re-layouts  10.8 us (6%)
  other arithmetic  4.13 us (2%)
    ppermute x32, waiting for transfers between devices, swap(): return lax.ppermute(v, axis, [(d, d ^ mask) for d in range(size)])  86.3 us
    ppermute x32, starting transfers between devices, swap(): return lax.ppermute(v, axis, [(d, d ^ mask) for d in range(size)])  43.6 us
    all_to_all x1, starting transfers between devices, route(): lax.all_to_all(sent.reshape(tiles * groups, depth, cols), ('tile', 'head'...  14.4 us
    pallas_call x1, Pallas kernels, body(): pl.pallas_call(attend_kernel, grid=(subs // PAIR,), in_specs=[pl.BlockSpe...  13.5 us
    unnamed x41, local copies, waits for them, and re-layouts  9.57 us
    pallas_call x1, Pallas kernels, route(): pl.pallas_call(functools.partial(route_kernel, spill), grid_spec=pltpu.Pr...  4.69 us
    pallas_call x1, Pallas kernels, body(): pl.pallas_call(prepare_kernel, grid=(1,), in_specs=[pl.BlockSpec(memory_s...  4.61 us
  transfers between devices with their start and end apart: 33, of which 18 were waited for; matrix products, arithmetic and copies ran while one was open for 2% of the time, Pallas kernels for 2%

commit v1 on v0

--- a/solution.py
+++ b/solution.py
@@ -384,7 +384,7 @@
             out[...] = result[d]
 
 
-def finish_kernel(place, r0, r1, r2, r3, lat, w_out, gain, w_inc, target, predicted, *grads):
+def finish_kernel(place, r0, r1, r2, r3, lat, w_out, gain, w_inc, target, *grads):
     width = lat.shape[1]
     heads = 8
     line = lax.broadcasted_iota(jnp.int32, (128, 2 * width), 0)
@@ -412,7 +412,6 @@
     power = jnp.mean(updated * updated, axis=1, keepdims=True)
     normed = (updated * lax.rsqrt(power + 1e-6) * gain[...]).astype(BF)
     answer = jnp.dot(normed, w_inc[...], preferred_element_type=F32)
-    predicted[...] = answer
     residual = answer - target[...].astype(F32)
     high = residual.astype(BF)
     low = (residual - high.astype(F32)).astype(BF)
@@ -420,11 +419,12 @@
     total = lax.dot_general(normed, high, dims, preferred_element_type=F32)
     total = total + lax.dot_general(normed, low, dims, preferred_element_type=F32)
     *grads, cut = grads
-    size = grads[0].shape[0]
+    size = cut.shape[1]
     for c in range(width // size):
         cut[c] = total[c * size:(c + 1) * size]
     for d, grad in enumerate(grads):
-        grad[...] = cut[place[0] ^ d]
+        grad[:size, :] = cut[place[0] ^ d]
+        grad[size:, :] = answer
 
 
 def body(
@@ -551,7 +551,9 @@
     starts = [sum(DEPTHS[:m]) for m in range(near)]
 
     def forward():
-        moved = [swap(v, "tile", m, tiles) for m, v in zip(NEAR, held)]
+        moved = [swap(v, "tile", m, tiles) for m, v in zip(NEAR[:-1], held[:-1])]
+        final, moved[0] = lax.optimization_barrier((held[-1], moved[0]))
+        moved.append(swap(final, "tile", NEAR[-1], tiles))
         return *moved, jnp.zeros((rest, groups, depth, cols), BF)
 
     def again():
@@ -599,7 +601,7 @@
         swap(partials[d], "head", d, groups) for d in range(1, groups)
     ]
     row = lambda *shape: pl.BlockSpec(shape, lambda i, m: (m[0], 0))
-    mine, *grads = pl.pallas_call(
+    terms = pl.pallas_call(
         finish_kernel,
         grid_spec=pltpu.PrefetchScalarGridSpec(
             num_scalar_prefetch=1,
@@ -612,11 +614,10 @@
                 whole(width, 128),
                 row(share, 128),
             ],
-            out_specs=[whole(share, 128)] + [whole(cols, 128)] * groups,
+            out_specs=[whole(cols + share, 128)] * groups,
             scratch_shapes=[pltpu.VMEM((groups, cols, 128), F32)],
         ),
-        out_shape=[jax.ShapeDtypeStruct((share, 128), F32)]
-        + [jax.ShapeDtypeStruct((cols, 128), F32)] * groups,
+        out_shape=[jax.ShapeDtypeStruct((cols + share, 128), F32)] * groups,
         compiler_params=pltpu.CompilerParams(vmem_limit_bytes=32 * 1024 * 1024),
         name="finish",
     )(
@@ -628,13 +629,13 @@
         w_inc,
         target,
     )
-    grads = [grads[0]] + [swap(grads[d], "head", d, groups) for d in range(1, groups)]
+    terms = [terms[0]] + [swap(terms[d], "head", d, groups) for d in range(1, groups)]
+    grads = [term[:cols] for term in terms]
     grad = (grads[0] + grads[1]) + (grads[2] + grads[3])
     for low, high in ((1, 2), (4, 8), (16, 32)):
         a, b, c = (swap(grad, "tile", m, tiles) for m in (low, high, low + high))
         grad = (grad + a) + (b + c)
-    preds = jnp.stack([mine] + [swap(mine, "head", d, groups) for d in range(1, groups)])
-    predicted = jnp.take(preds, turn, axis=0).reshape(lat_rows, 128)
+    predicted = jnp.take(jnp.stack([term[cols:] for term in terms]), turn, axis=0).reshape(lat_rows, 128)
     return predicted, grad * (1.0 / math.sqrt(lat_rows * tiles))
 
 

time: 189 us -> 185 us (0.979)
  starting transfers between devices: 58 us -> 51.5 us
  local copies, waits for them, and re-layouts: 10.8 us -> 14.3 us
    ppermute x32 -> x29, starting transfers between devices: 43.6 us -> 37.1 us  [swap(): return lax.ppermute(v, axis, [(d, d ^ mask) for d in range(size)])]
    unnamed x41 -> x45, local copies, waits for them, and re-layouts: 9.57 us -> 13.1 us
    ppermute x32 -> x29, waiting for transfers between devices: 86.3 us -> 85.4 us  [swap(): return lax.ppermute(v, axis, [(d, d ^ mask) for d in range(size)])]
  transfers between devices with their start and end apart: 33 -> 30, of which waited for: 18 -> 20; matrix products, arithmetic and copies ran while one was open for 2% -> 1% of each run, Pallas kernels for 2% -> 2%
where the time goes in v1:
time: 185 us; the launch traced here: 184 us
  waiting for transfers between devices  87.9 us (48%)
  starting transfers between devices  51.5 us (28%)
  Pallas kernels  25.4 us (14%)
  local copies, waits for them, and re-layouts  14.3 us (8%)
  other arithmetic  3.36 us (2%)
    ppermute x29, waiting for transfers between devices, swap(): return lax.ppermute(v, axis, [(d, d ^ mask) for d in range(size)])  85.4 us
    ppermute x29, starting transfers between devices, swap(): return lax.ppermute(v, axis, [(d, d ^ mask) for d in range(size)])  37.1 us
    all_to_all x1, starting transfers between devices, route(): lax.all_to_all(sent.reshape(tiles * groups, depth, cols), ('tile', 'head'...  14.4 us
    pallas_call x1, Pallas kernels, body(): pl.pallas_call(attend_kernel, grid=(subs // PAIR,), in_specs=[pl.BlockSpe...  13.8 us
    unnamed x45, local copies, waits for them, and re-layouts  13.1 us
    pallas_call x1, Pallas kernels, route(): pl.pallas_call(functools.partial(route_kernel, spill), grid_spec=pltpu.Pr...  4.73 us
  transfers between devices with their start and end apart: 30, of which 20 were waited for; matrix products, arithmetic and copies ran while one was open for 1% of the time, Pallas kernels for 2%

profile of v1, /device:TPU:32, one launch (start us, length us, event | category | flops | bytes accessed | tf_op | source)
XLA Modules:
  0.0 184.3 jit_solution(8599562084704983106)
XLA Ops:
  1.3 4.7 %route.3 = bf16[64,4,40,128]{3,2,1,0:T(8,128)(2,1)S(1)} custom-call(s32[64]{0:T(128)} %bitcast.51, s32[64]{0:T(128)S(1)} %reduce_max.9.alive, bf16[64,4,32,128]{3,2,1,0:T(8,128)(2,1)} %bitcast.43, s32[64,128]{1,0:T(8,128)} %bitcast.47, s32[16,64]{1,0:T(8,128)} %bitcast.49), custom_call_target="tpu_custom_call" | custom-call | tf_op jit(solution)/shard_map/route/pallas_call | solution.py:468
  6.1 1.5 copy-done
  7.6 14.4 %all-to-all-start.1 = ((bf16[256,40,128]{2,1,0:T(8,128)(2,1)}), bf16[256,40,128]{2,1,0:T(8,128)(2,1)S(1)}, u32[]{:S(2)}, u32[]{:S(2)}) async-start(bf16[256,40,128]{2,1,0:T(8,128)(2,1)} %bitcast.40), calls=%async_computation.1 | async-start | bytes 5242880 | tf_op jit(solution)/shard_map/all_to_all | solution.py:496
  22.1 1.0 pad_maximum_fusion.refs_4_
  23.2 1.6 collective-permute-start.11
  24.7 2.7 %collective-permute-start.12 = (bf16[512,512]{1,0:T(8,128)(2,1)S(1)}, bf16[512,512]{1,0:T(8,128)(2,1)S(1)}, u32[]{:S(2)}, u32[]{:S(2)}) collective-permute-start(bf16[512,512]{1,0:T(8,128)(2,1)S(1)} %pad_maximum_fusion.refs_4_), channel_id=1, source_target_pairs={{0,2},{1,3},{2,0},{3,1},{4,6},{5,7},{6,4},{7,5},{8,10},{9,11},{10,... | collective-permute-start | bytes 1572872 | tf_op jit(solution)/shard_map/ppermute | solution.py:461
  28.0 2.7 %collective-permute-start.10 = (f32[2]{0:T(128)S(1)}, f32[2]{0:T(128)S(1)}, u32[]{:S(2)}, u32[]{:S(2)}) collective-permute-start(f32[2]{0:T(128)S(1)} %copy-done.14), channel_id=1, source_target_pairs={{0,3},{1,2},{2,1},{3,0},{4,7},{5,6},{6,5},{7,4},{8,11},{9,10},{10,... | collective-permute-start | bytes 32 | tf_op jit(solution)/shard_map/ppermute | solution.py:461
  30.7 41.0 %collective-permute-done.10.refs_3_ = f32[2]{0:T(128)S(1)} collective-permute-done((f32[2]{0:T(128)S(1)}, f32[2]{0:T(128)S(1)}, u32[]{:S(2)}, u32[]{:S(2)}) %collective-permute-start.10) | collective-permute-done | bytes 40 | tf_op jit(solution)/shard_map/ppermute | solution.py:461
  71.7 5.0 %collective-permute-done.9.refs_2_ = f32[2]{0:T(128)S(1)} collective-permute-done((f32[2]{0:T(128)S(1)}, f32[2]{0:T(128)S(1)}, u32[]{:S(2)}, u32[]{:S(2)}) %collective-permute-start.9) | collective-permute-done | bytes 40 | tf_op jit(solution)/shard_map/ppermute | solution.py:461
  76.8 3.6 %prepare.1 = (bf16[8,512,512]{2,1,0:T(8,128)(2,1)S(1)}, f32[512,128]{1,0:T(8,128)S(1)}, f32[512,512]{1,0:T(8,128)S(1)}, bf16[512,512]{1,0:T(8,128)(2,1)S(1)}, bf16[512,512]{1,0:T(8,128)(2,1)S(1)}) custom-call(f32[2]{0:T(128)S(1)} %copy-done.14, f32[2]{0:T(128)S(1)} %collective-permute-done.8.refs_1_, f32[2]{0:T(128)S(1)} %collective-permute-done.9.refs_2_, ...), custom_call_target="tpu_custom_call" | custom-call | tf_op jit(solution)/shard_map/prepare/pallas_call | solution.py:511
  80.5 2.0 %copy-done.1 = bf16[8,512,512]{2,1,0:T(8,128)(2,1)} copy-done((bf16[8,512,512]{2,1,0:T(8,128)(2,1)}, bf16[8,512,512]{2,1,0:T(8,128)(2,1)S(1)}, u32[]{:S(2)}) %copy-start.1) | copy-done | bytes 4194328
  82.4 1.1 copy-done.3
  85.2 2.5 %all-to-all-done.1 = bf16[256,40,128]{2,1,0:T(8,128)(2,1)S(1)} async-done(((bf16[256,40,128]{2,1,0:T(8,128)(2,1)}), bf16[256,40,128]{2,1,0:T(8,128)(2,1)S(1)}, u32[]{:S(2)}, u32[]{:S(2)}) %all-to-all-start.1) | async-done | bytes 2621472 | tf_op jit(solution)/shard_map/all_to_all | solution.py:496
  87.7 1.8 plan.1
  90.7 20.3 %conditional.1 = (bf16[6,4,40,128]{3,2,1,0:T(8,128)(2,1)}, bf16[6,4,40,128]{3,2,1,0:T(8,128)(2,1)}, bf16[6,4,40,128]{3,2,1,0:T(8,128)(2,1)}, bf16[6,4,40,128]{3,...) conditional(s32[]{:T(128)} %bitcast.22, ...), branch_computations={%region_1.0_spmd, %region_2.0_spmd} | conditional | bytes 10485832 | solution.py:564
  91.0 1.8 collective-permute-start.2
  93.5 2.1 %collective-permute-start.4 = (bf16[6,4,40,128]{3,2,1,0:T(8,128)(2,1)S(1)}, bf16[6,4,40,128]{3,2,1,0:T(8,128)(2,1)}, u32[]{:S(2)}, u32[]{:S(2)}) collective-permute-start(bf16[6,4,40,128]{3,2,1,0:T(8,128)(2,1)S(1)} %get-tuple-element.37), channel_id=1, source_target_pairs={{0,196},{4,192},{8,204},{12,200},{16,212},{20,208},{24,220},{28,21... | collective-permute-start | bytes 737288 | tf_op jit(solution)/shard_map/cond/branch_1_fun/ppermute | solution.py:461
  95.6 1.2 collective-permute-start.5
  96.8 3.0 %collective-permute-done.1 = bf16[6,4,40,128]{3,2,1,0:T(8,128)(2,1)} collective-permute-done((bf16[6,4,40,128]{3,2,1,0:T(8,128)(2,1)S(1)}, bf16[6,4,40,128]{3,2,1,0:T(8,128)(2,1)}, u32[]{:S(2)}, u32[]{:S(2)}) %collective-permute-start.1) | collective-permute-done | bytes 245792 | tf_op jit(solution)/shard_map/cond/branch_1_fun/ppermute | solution.py:461
  99.8 4.3 %collective-permute-done.2 = bf16[6,4,40,128]{3,2,1,0:T(8,128)(2,1)} collective-permute-done((bf16[6,4,40,128]{3,2,1,0:T(8,128)(2,1)S(1)}, bf16[6,4,40,128]{3,2,1,0:T(8,128)(2,1)}, u32[]{:S(2)}, u32[]{:S(2)}) %collective-permute-start.2) | collective-permute-done | bytes 245792 | tf_op jit(solution)/shard_map/cond/branch_1_fun/ppermute | solution.py:461
  104.9 2.1 %collective-permute-done.4 = bf16[6,4,40,128]{3,2,1,0:T(8,128)(2,1)} collective-permute-done((bf16[6,4,40,128]{3,2,1,0:T(8,128)(2,1)S(1)}, bf16[6,4,40,128]{3,2,1,0:T(8,128)(2,1)}, u32[]{:S(2)}, u32[]{:S(2)}) %collective-permute-start.4) | collective-permute-done | bytes 245792 | tf_op jit(solution)/shard_map/cond/branch_1_fun/ppermute | solution.py:461
  107.0 1.9 %collective-permute-done.6 = bf16[6,4,40,128]{3,2,1,0:T(8,128)(2,1)} collective-permute-done((bf16[6,4,40,128]{3,2,1,0:T(8,128)(2,1)S(1)}, bf16[6,4,40,128]{3,2,1,0:T(8,128)(2,1)}, u32[]{:S(2)}, u32[]{:S(2)}) %collective-permute-start.6) | collective-permute-done | bytes 245792 | tf_op jit(solution)/shard_map/cond/branch_1_fun/ppermute | solution.py:461
  108.9 1.8 collective-permute-done.7
  111.0 0.9 copy-done.16
  111.9 1.2 copy-done.4
  113.2 1.0 copy-done.8
  114.2 13.8 %attend.1 = (bf16[128,640]{1,0:T(8,128)(2,1)S(1)}, bf16[128,640]{1,0:T(8,128)(2,1)}, bf16[128,640]{1,0:T(8,128)(2,1)}, bf16[128,640]{1,0:T(8,128)(2,1)}) custom-call(bf16[64,4,40,128]{3,2,1,0:T(8,128)(2,1)S(1)} %bitcast.39, bf16[6,4,40,128]{3,2,1,0:T(8,128)(2,1)} %get-tuple-element.83.refs_1_, bf16[6,4,40,128]{3,2,1,0:T(8,128)(2,1)} %get-tuple-element.84.refs_2_, ...), custom_call_target="tpu_custom_call" | custom-call | tf_op jit(solution)/shard_map/attend/pallas_call | solution.py:583
  129.2 1.5 collective-permute-start.15
  130.7 2.7 %collective-permute-start.16 = (bf16[128,640]{1,0:T(8,128)(2,1)}, bf16[128,640]{1,0:T(8,128)(2,1)S(1)}, u32[]{:S(2)}, u32[]{:S(2)}) collective-permute-start(bf16[128,640]{1,0:T(8,128)(2,1)} %get-tuple-element.99), channel_id=1, source_target_pairs={{0,3},{1,2},{2,1},{3,0},{4,7},{5,6},{6,5},{7,4},{8,11},{9,10},{10,... | collective-permute-start | bytes 491528 | tf_op jit(solution)/shard_map/ppermute | solution.py:461
  133.4 2.6 %collective-permute-done.14.r1 = bf16[128,640]{1,0:T(8,128)(2,1)S(1)} collective-permute-done((bf16[128,640]{1,0:T(8,128)(2,1)}, bf16[128,640]{1,0:T(8,128)(2,1)S(1)}, u32[]{:S(2)}, u32[]{:S(2)}) %collective-permute-start.14) | collective-permute-done | bytes 163872 | tf_op jit(solution)/shard_map/ppermute | solution.py:461
  136.0 2.5 %collective-permute-done.15.r2 = bf16[128,640]{1,0:T(8,128)(2,1)S(1)} collective-permute-done((bf16[128,640]{1,0:T(8,128)(2,1)}, bf16[128,640]{1,0:T(8,128)(2,1)S(1)}, u32[]{:S(2)}, u32[]{:S(2)}) %collective-permute-start.15) | collective-permute-done | bytes 163872 | tf_op jit(solution)/shard_map/ppermute | solution.py:461
  138.4 2.4 %collective-permute-done.16.r3 = bf16[128,640]{1,0:T(8,128)(2,1)S(1)} collective-permute-done((bf16[128,640]{1,0:T(8,128)(2,1)}, bf16[128,640]{1,0:T(8,128)(2,1)S(1)}, u32[]{:S(2)}, u32[]{:S(2)}) %collective-permute-start.16) | collective-permute-done | bytes 163872 | tf_op jit(solution)/shard_map/ppermute | solution.py:461
  140.9 1.0 copy-done.6
  141.9 0.9 copy-done.10
  143.7 1.4 finish.1
  145.2 4.1 %collective-permute-start.18 = (f32[256,128]{1,0:T(8,128)S(1)}, f32[256,128]{1,0:T(8,128)S(1)}, u32[]{:S(2)}, u32[]{:S(2)}) collective-permute-start(f32[256,128]{1,0:T(8,128)S(1)} %get-tuple-element.103), channel_id=1, source_target_pairs={{0,2},{1,3},{2,0},{3,1},{4,6},{5,7},{6,4},{7,5},{8,10},{9,11},{10,... | collective-permute-start | bytes 393224 | tf_op jit(solution)/shard_map/ppermute | solution.py:461
  150.0 1.4 collective-permute-done.17
  151.4 3.4 %collective-permute-done.18 = f32[256,128]{1,0:T(8,128)S(1)} collective-permute-done((f32[256,128]{1,0:T(8,128)S(1)}, f32[256,128]{1,0:T(8,128)S(1)}, u32[]{:S(2)}, u32[]{:S(2)}) %collective-permute-start.18) | collective-permute-done | bytes 131104 | tf_op jit(solution)/shard_map/ppermute | solution.py:461
  154.8 1.7 collective-permute-done.19
  156.7 1.3 collective-permute-start.21
  158.6 3.0 %collective-permute-done.21 = f32[128,128]{1,0:T(8,128)S(1)} collective-permute-done((f32[128,128]{1,0:T(8,128)S(1)}, f32[128,128]{1,0:T(8,128)S(1)}, u32[]{:S(2)}, u32[]{:S(2)}) %collective-permute-start.21) | collective-permute-done | bytes 65568 | tf_op jit(solution)/shard_map/ppermute | solution.py:461
  162.8 3.5 %collective-permute-start.24 = (f32[128,128]{1,0:T(8,128)S(1)}, f32[128,128]{1,0:T(8,128)S(1)}, u32[]{:S(2)}, u32[]{:S(2)}) collective-permute-start(f32[128,128]{1,0:T(8,128)S(1)} %add_add_fusion.1), channel_id=1, source_target_pairs={{0,32},{4,36},{8,40},{12,44},{16,48},{20,52},{24,56},{28,60},{32,0... | collective-permute-start | bytes 196616 | tf_op jit(solution)/shard_map/ppermute | solution.py:461
  166.3 2.7 %collective-permute-start.25 = (f32[128,128]{1,0:T(8,128)S(1)}, f32[128,128]{1,0:T(8,128)S(1)}, u32[]{:S(2)}, u32[]{:S(2)}) collective-permute-start(f32[128,128]{1,0:T(8,128)S(1)} %add_add_fusion.1), channel_id=1, source_target_pairs={{0,48},{4,52},{8,56},{12,60},{16,32},{20,36},{24,40},{28,44},{32,1... | collective-permute-start | bytes 196616 | tf_op jit(solution)/shard_map/ppermute | solution.py:461
  169.5 1.6 collective-permute-done.24
  171.1 4.4 %collective-permute-done.25 = f32[128,128]{1,0:T(8,128)S(1)} collective-permute-done((f32[128,128]{1,0:T(8,128)S(1)}, f32[128,128]{1,0:T(8,128)S(1)}, u32[]{:S(2)}, u32[]{:S(2)}) %collective-permute-start.25) | collective-permute-done | bytes 65568 | tf_op jit(solution)/shard_map/ppermute | solution.py:461
  175.7 2.4 %collective-permute-start.27 = (f32[128,128]{1,0:T(8,128)S(1)}, f32[128,128]{1,0:T(8,128)S(1)}, u32[]{:S(2)}, u32[]{:S(2)}) collective-permute-start(f32[128,128]{1,0:T(8,128)S(1)} %add_add_fusion), channel_id=1, source_target_pairs={{0,128},{4,132},{8,136},{12,140},{16,144},{20,148},{24,152},{28,15... | collective-permute-start | bytes 196616 | tf_op jit(solution)/shard_map/ppermute | solution.py:461
  178.1 2.2 %collective-permute-start.28 = (f32[128,128]{1,0:T(8,128)S(1)}, f32[128,128]{1,0:T(8,128)S(1)}, u32[]{:S(2)}, u32[]{:S(2)}) collective-permute-start(f32[128,128]{1,0:T(8,128)S(1)} %add_add_fusion), channel_id=1, source_target_pairs={{0,192},{4,196},{8,200},{12,204},{16,208},{20,212},{24,216},{28,22... | collective-permute-start | bytes 196616 | tf_op jit(solution)/shard_map/ppermute | solution.py:461
  181.9 1.7 collective-permute-done.28
  (78 shorter events, 13.2 us)
Async XLA Ops:
  6.1 1.5 copy-start
  7.6 14.4 %copy-start.18 = (bf16[128,512]{1,0:T(8,128)(2,1)S(1)}, bf16[128,512]{1,0:T(8,128)(2,1)}, u32[]{:S(2)}) copy-start(bf16[128,512]{1,0:T(8,128)(2,1)} %param.24) | copy-start | bytes 393220
  7.6 14.5 %copy-start.19 = (bf16[512,128]{1,0:T(8,128)(2,1)S(1)}, bf16[512,128]{1,0:T(8,128)(2,1)}, u32[]{:S(2)}) copy-start(bf16[512,128]{1,0:T(8,128)(2,1)} %param.22) | copy-start | bytes 393220
  7.6 20.4 %copy-start.14 = (f32[2]{0:T(128)S(1)}, f32[2]{0:T(128)}, u32[]{:S(2)}) copy-start(f32[2]{0:T(128)} %refs_0_.1) | copy-start | bytes 28
  7.6 69.2 %copy-start.2 = (bf16[512,512]{1,0:T(8,128)(2,1)S(1)}, bf16[512,512]{1,0:T(8,128)(2,1)}, u32[]{:S(2)}) copy-start(bf16[512,512]{1,0:T(8,128)(2,1)} %lat.1) | copy-start | bytes 1572868
  7.6 80.1 %all-to-all-start.1 = ((bf16[256,40,128]{2,1,0:T(8,128)(2,1)}), bf16[256,40,128]{2,1,0:T(8,128)(2,1)S(1)}, u32[]{:S(2)}, u32[]{:S(2)}) async-start(bf16[256,40,128]{2,1,0:T(8,128)(2,1)} %bitcast.40), calls=%async_computation.1 | async-start | bytes 5242880 | tf_op jit(solution)/shard_map/all_to_all | solution.py:496
  23.2 53.6 %collective-permute-start.11 = (bf16[512,512]{1,0:T(8,128)(2,1)S(1)}, bf16[512,512]{1,0:T(8,128)(2,1)S(1)}, u32[]{:S(2)}, u32[]{:S(2)}) collective-permute-start(bf16[512,512]{1,0:T(8,128)(2,1)S(1)} %pad_maximum_fusion.refs_4_), channel_id=1, source_target_pairs={{0,1},{1,0},{2,3},{3,2},{4,5},{5,4},{6,7},{7,6},{8,9},{9,8},{10,11... | collective-permute-start | bytes 1572872 | tf_op jit(solution)/shard_map/ppermute | solution.py:461
  24.7 52.0 %collective-permute-start.12 = (bf16[512,512]{1,0:T(8,128)(2,1)S(1)}, bf16[512,512]{1,0:T(8,128)(2,1)S(1)}, u32[]{:S(2)}, u32[]{:S(2)}) collective-permute-start(bf16[512,512]{1,0:T(8,128)(2,1)S(1)} %pad_maximum_fusion.refs_4_), channel_id=1, source_target_pairs={{0,2},{1,3},{2,0},{3,1},{4,6},{5,7},{6,4},{7,5},{8,10},{9,11},{10,... | collective-permute-start | bytes 1572872 | tf_op jit(solution)/shard_map/ppermute | solution.py:461
  27.5 49.3 %collective-permute-start.13 = (bf16[512,512]{1,0:T(8,128)(2,1)S(1)}, bf16[512,512]{1,0:T(8,128)(2,1)S(1)}, u32[]{:S(2)}, u32[]{:S(2)}) collective-permute-start(bf16[512,512]{1,0:T(8,128)(2,1)S(1)} %pad_maximum_fusion.refs_4_), channel_id=1, source_target_pairs={{0,3},{1,2},{2,1},{3,0},{4,7},{5,6},{6,5},{7,4},{8,11},{9,10},{10,... | collective-permute-start | bytes 1572872 | tf_op jit(solution)/shard_map/ppermute | solution.py:461
  28.0 43.8 %collective-permute-start.10 = (f32[2]{0:T(128)S(1)}, f32[2]{0:T(128)S(1)}, u32[]{:S(2)}, u32[]{:S(2)}) collective-permute-start(f32[2]{0:T(128)S(1)} %copy-done.14), channel_id=1, source_target_pairs={{0,3},{1,2},{2,1},{3,0},{4,7},{5,6},{6,5},{7,4},{8,11},{9,10},{10,... | collective-permute-start | bytes 32 | tf_op jit(solution)/shard_map/ppermute | solution.py:461
  30.7 41.0 %collective-permute-start.8 = (f32[2]{0:T(128)S(1)}, f32[2]{0:T(128)S(1)}, u32[]{:S(2)}, u32[]{:S(2)}) collective-permute-start(f32[2]{0:T(128)S(1)} %copy-done.14), channel_id=1, source_target_pairs={{0,1},{1,0},{2,3},{3,2},{4,5},{5,4},{6,7},{7,6},{8,9},{9,8},{10,11... | collective-permute-start | bytes 32 | tf_op jit(solution)/shard_map/ppermute | solution.py:461
  30.7 60.0 %copy-start.17 = (s32[8192]{0:T(1024)S(1)}, s32[8192]{0:T(1024)}, u32[]{:S(2)}) copy-start(s32[8192]{0:T(1024)} %param.16) | copy-start | bytes 98308
  30.7 60.0 %copy-start.20 = (s32[64,16]{0,1:T(8,128)S(1)}, s32[64,16]{0,1:T(8,128)}, u32[]{:S(2)}) copy-start(s32[64,16]{0,1:T(8,128)} %param.18) | copy-start | bytes 12292
  30.7 60.0 %copy-start.21 = (s32[64,1]{0,1:T(1,128)S(1)}, s32[64,1]{0,1:T(1,128)}, u32[]{:S(2)}) copy-start(s32[64,1]{0,1:T(1,128)} %param.17) | copy-start | bytes 772
  71.7 5.0 %collective-permute-start.9 = (f32[2]{0:T(128)S(1)}, f32[2]{0:T(128)S(1)}, u32[]{:S(2)}, u32[]{:S(2)}) collective-permute-start(f32[2]{0:T(128)S(1)} %copy-done.14), channel_id=1, source_target_pairs={{0,2},{1,3},{2,0},{3,1},{4,6},{5,7},{6,4},{7,5},{8,10},{9,11},{10,... | collective-permute-start | bytes 32 | tf_op jit(solution)/shard_map/ppermute | solution.py:461
  80.4 2.0 %copy-start.1 = (bf16[8,512,512]{2,1,0:T(8,128)(2,1)}, bf16[8,512,512]{2,1,0:T(8,128)(2,1)S(1)}, u32[]{:S(2)}) copy-start(bf16[8,512,512]{2,1,0:T(8,128)(2,1)S(1)} %get-tuple-element.92.refs_10_) | copy-start | bytes 12582916
  82.4 1.1 copy-start.3
  87.7 3.0 %copy-start.15 = (bf16[8192,128]{1,0:T(8,128)(2,1)S(1)}, bf16[8192,128]{1,0:T(8,128)(2,1)}, u32[]{:S(2)}) copy-start(bf16[8192,128]{1,0:T(8,128)(2,1)} %param.15) | copy-start | bytes 6291460
  90.8 4.9 %collective-permute-start = (bf16[6,4,40,128]{3,2,1,0:T(8,128)(2,1)S(1)}, bf16[6,4,40,128]{3,2,1,0:T(8,128)(2,1)}, u32[]{:S(2)}, u32[]{:S(2)}) collective-permute-start(bf16[6,4,40,128]{3,2,1,0:T(8,128)(2,1)S(1)} %get-tuple-element.32), channel_id=1, source_target_pairs={{0,4},{4,0},{8,12},{12,8},{16,20},{20,16},{24,28},{28,24},{32,36},... | collective-permute-start | bytes 737288 | tf_op jit(solution)/shard_map/cond/branch_1_fun/ppermute | solution.py:461
  90.9 9.0 %collective-permute-start.1 = (bf16[6,4,40,128]{3,2,1,0:T(8,128)(2,1)S(1)}, bf16[6,4,40,128]{3,2,1,0:T(8,128)(2,1)}, u32[]{:S(2)}, u32[]{:S(2)}) collective-permute-start(bf16[6,4,40,128]{3,2,1,0:T(8,128)(2,1)S(1)} %get-tuple-element.34), channel_id=1, source_target_pairs={{0,64},{4,68},{8,72},{12,76},{16,80},{20,84},{24,88},{28,92},{32,9... | collective-permute-start | bytes 737288 | tf_op jit(solution)/shard_map/cond/branch_1_fun/ppermute | solution.py:461
  91.0 13.2 %collective-permute-start.2 = (bf16[6,4,40,128]{3,2,1,0:T(8,128)(2,1)S(1)}, bf16[6,4,40,128]{3,2,1,0:T(8,128)(2,1)}, u32[]{:S(2)}, u32[]{:S(2)}) collective-permute-start(bf16[6,4,40,128]{3,2,1,0:T(8,128)(2,1)S(1)} %get-tuple-element.35), channel_id=1, source_target_pairs={{0,68},{4,64},{8,76},{12,72},{16,84},{20,80},{24,92},{28,88},{32,1... | collective-permute-start | bytes 737288 | tf_op jit(solution)/shard_map/cond/branch_1_fun/ppermute | solution.py:461
  92.7 12.1 %collective-permute-start.3 = (bf16[6,4,40,128]{3,2,1,0:T(8,128)(2,1)S(1)}, bf16[6,4,40,128]{3,2,1,0:T(8,128)(2,1)}, u32[]{:S(2)}, u32[]{:S(2)}) collective-permute-start(bf16[6,4,40,128]{3,2,1,0:T(8,128)(2,1)S(1)} %get-tuple-element.36), channel_id=1, source_target_pairs={{0,192},{4,196},{8,200},{12,204},{16,208},{20,212},{24,216},{28,22... | collective-permute-start | bytes 737288 | tf_op jit(solution)/shard_map/cond/branch_1_fun/ppermute | solution.py:461
  93.5 13.4 %collective-permute-start.4 = (bf16[6,4,40,128]{3,2,1,0:T(8,128)(2,1)S(1)}, bf16[6,4,40,128]{3,2,1,0:T(8,128)(2,1)}, u32[]{:S(2)}, u32[]{:S(2)}) collective-permute-start(bf16[6,4,40,128]{3,2,1,0:T(8,128)(2,1)S(1)} %get-tuple-element.37), channel_id=1, source_target_pairs={{0,196},{4,192},{8,204},{12,200},{16,212},{20,208},{24,220},{28,21... | collective-permute-start | bytes 737288 | tf_op jit(solution)/shard_map/cond/branch_1_fun/ppermute | solution.py:461
  95.6 11.3 %collective-permute-start.5 = (bf16[6,4,40,128]{3,2,1,0:T(8,128)(2,1)S(1)}, bf16[6,4,40,128]{3,2,1,0:T(8,128)(2,1)}, u32[]{:S(2)}, u32[]{:S(2)}) collective-permute-start(bf16[6,4,40,128]{3,2,1,0:T(8,128)(2,1)S(1)} %get-tuple-element.38), channel_id=1, source_target_pairs={{0,8},{4,12},{8,0},{12,4},{16,24},{20,28},{24,16},{28,20},{32,40},... | collective-permute-start | bytes 737288 | tf_op jit(solution)/shard_map/cond/branch_1_fun/ppermute | solution.py:461
  99.8 9.1 %collective-permute-start.6 = (bf16[6,4,40,128]{3,2,1,0:T(8,128)(2,1)S(1)}, bf16[6,4,40,128]{3,2,1,0:T(8,128)(2,1)}, u32[]{:S(2)}, u32[]{:S(2)}) collective-permute-start(bf16[6,4,40,128]{3,2,1,0:T(8,128)(2,1)S(1)} %get-tuple-element.39), channel_id=1, source_target_pairs={{0,12},{4,8},{8,4},{12,0},{16,28},{20,24},{24,20},{28,16},{32,44},... | collective-permute-start | bytes 737288 | tf_op jit(solution)/shard_map/cond/branch_1_fun/ppermute | solution.py:461
  104.1 6.6 %collective-permute-start.7 = (bf16[2,4,40,128]{3,2,1,0:T(8,128)(2,1)S(1)}, bf16[2,4,40,128]{3,2,1,0:T(8,128)(2,1)}, u32[]{:S(2)}, u32[]{:S(2)}) collective-permute-start(bf16[2,4,40,128]{3,2,1,0:T(8,128)(2,1)S(1)} %get-tuple-element.40), channel_id=1, source_target_pairs={{0,128},{4,132},{8,136},{12,140},{16,144},{20,148},{24,152},{28,15... | collective-permute-start | bytes 245768 | tf_op jit(solution)/shard_map/cond/branch_1_fun/ppermute | solution.py:461
  111.0 0.9 copy-start.16
  111.9 1.2 copy-start.4
  113.2 1.0 copy-start.8
  114.2 26.7 %copy-start.11 = (bf16[512,128]{1,0:T(8,128)(2,1)S(1)}, bf16[512,128]{1,0:T(8,128)(2,1)}, u32[]{:S(2)}) copy-start(bf16[512,128]{1,0:T(8,128)(2,1)} %w_inc.1) | copy-start | bytes 393220
  114.2 26.7 %copy-start.13 = (f32[512]{0:T(512)S(1)}, f32[512]{0:T(512)}, u32[]{:S(2)}) copy-start(f32[512]{0:T(512)} %param.25) | copy-start | bytes 6148
  128.7 7.3 %collective-permute-start.14 = (bf16[128,640]{1,0:T(8,128)(2,1)}, bf16[128,640]{1,0:T(8,128)(2,1)S(1)}, u32[]{:S(2)}, u32[]{:S(2)}) collective-permute-start(bf16[128,640]{1,0:T(8,128)(2,1)} %get-tuple-element.97), channel_id=1, source_target_pairs={{0,1},{1,0},{2,3},{3,2},{4,5},{5,4},{6,7},{7,6},{8,9},{9,8},{10,11... | collective-permute-start | bytes 491528 | tf_op jit(solution)/shard_map/ppermute | solution.py:461
  129.2 9.2 %collective-permute-start.15 = (bf16[128,640]{1,0:T(8,128)(2,1)}, bf16[128,640]{1,0:T(8,128)(2,1)S(1)}, u32[]{:S(2)}, u32[]{:S(2)}) collective-permute-start(bf16[128,640]{1,0:T(8,128)(2,1)} %get-tuple-element.98), channel_id=1, source_target_pairs={{0,2},{1,3},{2,0},{3,1},{4,6},{5,7},{6,4},{7,5},{8,10},{9,11},{10,... | collective-permute-start | bytes 491528 | tf_op jit(solution)/shard_map/ppermute | solution.py:461
  130.7 10.2 %collective-permute-start.16 = (bf16[128,640]{1,0:T(8,128)(2,1)}, bf16[128,640]{1,0:T(8,128)(2,1)S(1)}, u32[]{:S(2)}, u32[]{:S(2)}) collective-permute-start(bf16[128,640]{1,0:T(8,128)(2,1)} %get-tuple-element.99), channel_id=1, source_target_pairs={{0,3},{1,2},{2,1},{3,0},{4,7},{5,6},{6,5},{7,4},{8,11},{9,10},{10,... | collective-permute-start | bytes 491528 | tf_op jit(solution)/shard_map/ppermute | solution.py:461
  140.9 1.0 copy-start.6
  141.9 0.9 copy-start.10
  145.1 6.3 %collective-permute-start.17 = (f32[256,128]{1,0:T(8,128)S(1)}, f32[256,128]{1,0:T(8,128)S(1)}, u32[]{:S(2)}, u32[]{:S(2)}) collective-permute-start(f32[256,128]{1,0:T(8,128)S(1)} %get-tuple-element.102), channel_id=1, source_target_pairs={{0,1},{1,0},{2,3},{3,2},{4,5},{5,4},{6,7},{7,6},{8,9},{9,8},{10,11... | collective-permute-start | bytes 393224 | tf_op jit(solution)/shard_map/ppermute | solution.py:461
  145.2 9.6 %collective-permute-start.18 = (f32[256,128]{1,0:T(8,128)S(1)}, f32[256,128]{1,0:T(8,128)S(1)}, u32[]{:S(2)}, u32[]{:S(2)}) collective-permute-start(f32[256,128]{1,0:T(8,128)S(1)} %get-tuple-element.103), channel_id=1, source_target_pairs={{0,2},{1,3},{2,0},{3,1},{4,6},{5,7},{6,4},{7,5},{8,10},{9,11},{10,... | collective-permute-start | bytes 393224 | tf_op jit(solution)/shard_map/ppermute | solution.py:461
  149.4 7.2 %collective-permute-start.19 = (f32[256,128]{1,0:T(8,128)S(1)}, f32[256,128]{1,0:T(8,128)S(1)}, u32[]{:S(2)}, u32[]{:S(2)}) collective-permute-start(f32[256,128]{1,0:T(8,128)S(1)} %get-tuple-element.104), channel_id=1, source_target_pairs={{0,3},{1,2},{2,1},{3,0},{4,7},{5,6},{6,5},{7,4},{8,11},{9,10},{10,... | collective-permute-start | bytes 393224 | tf_op jit(solution)/shard_map/ppermute | solution.py:461
  156.6 2.0 %collective-permute-start.20 = (f32[128,128]{1,0:T(8,128)S(1)}, f32[128,128]{1,0:T(8,128)S(1)}, u32[]{:S(2)}, u32[]{:S(2)}) collective-permute-start(f32[128,128]{1,0:T(8,128)S(1)} %get-tuple-element.112), channel_id=1, source_target_pairs={{0,4},{4,0},{8,12},{12,8},{16,20},{20,16},{24,28},{28,24},{32,36},... | collective-permute-start | bytes 196616 | tf_op jit(solution)/shard_map/ppermute | solution.py:461
  156.7 4.8 %collective-permute-start.21 = (f32[128,128]{1,0:T(8,128)S(1)}, f32[128,128]{1,0:T(8,128)S(1)}, u32[]{:S(2)}, u32[]{:S(2)}) collective-permute-start(f32[128,128]{1,0:T(8,128)S(1)} %get-tuple-element.112), channel_id=1, source_target_pairs={{0,8},{4,12},{8,0},{12,4},{16,24},{20,28},{24,16},{28,20},{32,40},... | collective-permute-start | bytes 196616 | tf_op jit(solution)/shard_map/ppermute | solution.py:461
  158.0 4.3 %collective-permute-start.22 = (f32[128,128]{1,0:T(8,128)S(1)}, f32[128,128]{1,0:T(8,128)S(1)}, u32[]{:S(2)}, u32[]{:S(2)}) collective-permute-start(f32[128,128]{1,0:T(8,128)S(1)} %get-tuple-element.112), channel_id=1, source_target_pairs={{0,12},{4,8},{8,4},{12,0},{16,28},{20,24},{24,20},{28,16},{32,44},... | collective-permute-start | bytes 196616 | tf_op jit(solution)/shard_map/ppermute | solution.py:461
  162.3 7.2 %collective-permute-start.23 = (f32[128,128]{1,0:T(8,128)S(1)}, f32[128,128]{1,0:T(8,128)S(1)}, u32[]{:S(2)}, u32[]{:S(2)}) collective-permute-start(f32[128,128]{1,0:T(8,128)S(1)} %add_add_fusion.1), channel_id=1, source_target_pairs={{0,16},{4,20},{8,24},{12,28},{16,0},{20,4},{24,8},{28,12},{32,48},... | collective-permute-start | bytes 196616 | tf_op jit(solution)/shard_map/ppermute | solution.py:461
  162.8 8.3 %collective-permute-start.24 = (f32[128,128]{1,0:T(8,128)S(1)}, f32[128,128]{1,0:T(8,128)S(1)}, u32[]{:S(2)}, u32[]{:S(2)}) collective-permute-start(f32[128,128]{1,0:T(8,128)S(1)} %add_add_fusion.1), channel_id=1, source_target_pairs={{0,32},{4,36},{8,40},{12,44},{16,48},{20,52},{24,56},{28,60},{32,0... | collective-permute-start | bytes 196616 | tf_op jit(solution)/shard_map/ppermute | solution.py:461
  166.3 9.3 %collective-permute-start.25 = (f32[128,128]{1,0:T(8,128)S(1)}, f32[128,128]{1,0:T(8,128)S(1)}, u32[]{:S(2)}, u32[]{:S(2)}) collective-permute-start(f32[128,128]{1,0:T(8,128)S(1)} %add_add_fusion.1), channel_id=1, source_target_pairs={{0,48},{4,52},{8,56},{12,60},{16,32},{20,36},{24,40},{28,44},{32,1... | collective-permute-start | bytes 196616 | tf_op jit(solution)/shard_map/ppermute | solution.py:461
  175.6 5.6 %collective-permute-start.26 = (f32[128,128]{1,0:T(8,128)S(1)}, f32[128,128]{1,0:T(8,128)S(1)}, u32[]{:S(2)}, u32[]{:S(2)}) collective-permute-start(f32[128,128]{1,0:T(8,128)S(1)} %add_add_fusion), channel_id=1, source_target_pairs={{0,64},{4,68},{8,72},{12,76},{16,80},{20,84},{24,88},{28,92},{32,9... | collective-permute-start | bytes 196616 | tf_op jit(solution)/shard_map/ppermute | solution.py:461
  175.7 6.2 %collective-permute-start.27 = (f32[128,128]{1,0:T(8,128)S(1)}, f32[128,128]{1,0:T(8,128)S(1)}, u32[]{:S(2)}, u32[]{:S(2)}) collective-permute-start(f32[128,128]{1,0:T(8,128)S(1)} %add_add_fusion), channel_id=1, source_target_pairs={{0,128},{4,132},{8,136},{12,140},{16,144},{20,148},{24,152},{28,15... | collective-permute-start | bytes 196616 | tf_op jit(solution)/shard_map/ppermute | solution.py:461
  178.1 5.5 %collective-permute-start.28 = (f32[128,128]{1,0:T(8,128)S(1)}, f32[128,128]{1,0:T(8,128)S(1)}, u32[]{:S(2)}, u32[]{:S(2)}) collective-permute-start(f32[128,128]{1,0:T(8,128)S(1)} %add_add_fusion), channel_id=1, source_target_pairs={{0,192},{4,196},{8,200},{12,204},{16,208},{20,212},{24,216},{28,22... | collective-permute-start | bytes 196616 | tf_op jit(solution)/shard_map/ppermute | solution.py:461
  (4 other events, 3.2 us)

commit v2 on v1

--- a/solution.py
+++ b/solution.py
@@ -484,7 +484,7 @@
                 ],
             ),
             out_shape=jax.ShapeDtypeStruct((tiles, groups, depth, cols), BF),
-            compiler_params=pltpu.CompilerParams(vmem_limit_bytes=32 * 1024 * 1024),
+            compiler_params=pltpu.CompilerParams(vmem_limit_bytes=20 * 1024 * 1024),
             name="route",
         )(
             block_owner[:, 0],
@@ -528,7 +528,7 @@
             jax.ShapeDtypeStruct((width, width), BF),
             jax.ShapeDtypeStruct((width, width), BF),
         ],
-        compiler_params=pltpu.CompilerParams(vmem_limit_bytes=32 * 1024 * 1024),
+        compiler_params=pltpu.CompilerParams(vmem_limit_bytes=28 * 1024 * 1024),
         name="prepare",
     )(*biases, *nearby, latent)
 
@@ -544,7 +544,7 @@
             pltpu.SMEM((2 * near, 128), jnp.int32),
             pltpu.SemaphoreType.DMA,
         ],
-        compiler_params=pltpu.CompilerParams(vmem_limit_bytes=32 * 1024 * 1024),
+        compiler_params=pltpu.CompilerParams(vmem_limit_bytes=20 * 1024 * 1024),
         name="plan",
     )(arrived)
     rest = tiles - sum(DEPTHS)
@@ -593,7 +593,7 @@
         out_specs=[whole(share, width + 128)] * groups,
         scratch_shapes=scratch,
         out_shape=[jax.ShapeDtypeStruct((share, width + 128), BF)] * groups,
-        compiler_params=pltpu.CompilerParams(vmem_limit_bytes=48 * 1024 * 1024),
+        compiler_params=pltpu.CompilerParams(vmem_limit_bytes=30 * 1024 * 1024),
         name="attend",
     )(*units, qw, states, numer, wv)
 
@@ -618,7 +618,7 @@
             scratch_shapes=[pltpu.VMEM((groups, cols, 128), F32)],
         ),
         out_shape=[jax.ShapeDtypeStruct((cols + share, 128), F32)] * groups,
-        compiler_params=pltpu.CompilerParams(vmem_limit_bytes=32 * 1024 * 1024),
+        compiler_params=pltpu.CompilerParams(vmem_limit_bytes=16 * 1024 * 1024),
         name="finish",
     )(
         me[None].astype(jnp.int32),

time: 185 us -> 186 us (level)
  local copies, waits for them, and re-layouts: 14.3 us -> 16.5 us
    unnamed x45 -> x47, local copies, waits for them, and re-layouts: 13.1 us -> 15.3 us
where the time goes in v2:
time: 186 us; the launch traced here: 185 us
  waiting for transfers between devices  87.9 us (47%)
  starting transfers between devices  51.5 us (28%)
  Pallas kernels  24.1 us (13%)
  local copies, waits for them, and re-layouts  16.5 us (9%)
  other arithmetic  3.36 us (2%)
    ppermute x29, waiting for transfers between devices, swap(): return lax.ppermute(v, axis, [(d, d ^ mask) for d in range(size)])  85.4 us
    ppermute x29, starting transfers between devices, swap(): return lax.ppermute(v, axis, [(d, d ^ mask) for d in range(size)])  37.1 us
    unnamed x47, local copies, waits for them, and re-layouts  15.3 us
    all_to_all x1, starting transfers between devices, route(): lax.all_to_all(sent.reshape(tiles * groups, depth, cols), ('tile', 'head'...  14.4 us
    pallas_call x1, Pallas kernels, body(): pl.pallas_call(attend_kernel, grid=(subs // PAIR,), in_specs=[pl.BlockSpe...  12.5 us
    pallas_call x1, Pallas kernels, route(): pl.pallas_call(functools.partial(route_kernel, spill), grid_spec=pltpu.Pr...  4.73 us
  transfers between devices with their start and end apart: 30, of which 20 were waited for; matrix products, arithmetic and copies ran while one was open for 1% of the time, Pallas kernels for 2%

profile of v2, /device:TPU:32, one launch (start us, length us, event | category | flops | bytes accessed | tf_op | source)
XLA Modules:
  0.0 185.2 jit_solution(15475889533984620635)
XLA Ops:
  1.3 4.7 %route.3 = bf16[64,4,40,128]{3,2,1,0:T(8,128)(2,1)S(1)} custom-call(s32[64]{0:T(128)} %bitcast.51, s32[64]{0:T(128)S(1)} %reduce_max.9.alive, bf16[64,4,32,128]{3,2,1,0:T(8,128)(2,1)} %bitcast.43, s32[64,128]{1,0:T(8,128)} %bitcast.47, s32[16,64]{1,0:T(8,128)} %bitcast.49), custom_call_target="tpu_custom_call" | custom-call | tf_op jit(solution)/shard_map/route/pallas_call | solution.py:468
  6.1 1.5 copy-done
  7.6 14.4 %all-to-all-start.1 = ((bf16[256,40,128]{2,1,0:T(8,128)(2,1)}), bf16[256,40,128]{2,1,0:T(8,128)(2,1)S(1)}, u32[]{:S(2)}, u32[]{:S(2)}) async-start(bf16[256,40,128]{2,1,0:T(8,128)(2,1)} %bitcast.40), calls=%async_computation.1 | async-start | bytes 5242880 | tf_op jit(solution)/shard_map/all_to_all | solution.py:496
  22.2 1.0 pad_maximum_fusion.refs_4_
  23.2 1.6 collective-permute-start.11
  24.8 2.7 %collective-permute-start.12 = (bf16[512,512]{1,0:T(8,128)(2,1)S(1)}, bf16[512,512]{1,0:T(8,128)(2,1)S(1)}, u32[]{:S(2)}, u32[]{:S(2)}) collective-permute-start(bf16[512,512]{1,0:T(8,128)(2,1)S(1)} %pad_maximum_fusion.refs_4_), channel_id=1, source_target_pairs={{0,2},{1,3},{2,0},{3,1},{4,6},{5,7},{6,4},{7,5},{8,10},{9,11},{10,... | collective-permute-start | bytes 1572872 | tf_op jit(solution)/shard_map/ppermute | solution.py:461
  28.0 2.7 %collective-permute-start.10 = (f32[2]{0:T(128)S(1)}, f32[2]{0:T(128)S(1)}, u32[]{:S(2)}, u32[]{:S(2)}) collective-permute-start(f32[2]{0:T(128)S(1)} %copy-done.15), channel_id=1, source_target_pairs={{0,3},{1,2},{2,1},{3,0},{4,7},{5,6},{6,5},{7,4},{8,11},{9,10},{10,... | collective-permute-start | bytes 32 | tf_op jit(solution)/shard_map/ppermute | solution.py:461
  30.7 41.0 %collective-permute-done.10.refs_3_ = f32[2]{0:T(128)S(1)} collective-permute-done((f32[2]{0:T(128)S(1)}, f32[2]{0:T(128)S(1)}, u32[]{:S(2)}, u32[]{:S(2)}) %collective-permute-start.10) | collective-permute-done | bytes 40 | tf_op jit(solution)/shard_map/ppermute | solution.py:461
  71.8 5.0 %collective-permute-done.9.refs_2_ = f32[2]{0:T(128)S(1)} collective-permute-done((f32[2]{0:T(128)S(1)}, f32[2]{0:T(128)S(1)}, u32[]{:S(2)}, u32[]{:S(2)}) %collective-permute-start.9) | collective-permute-done | bytes 40 | tf_op jit(solution)/shard_map/ppermute | solution.py:461
  76.8 3.6 %prepare.1 = (bf16[8,512,512]{2,1,0:T(8,128)(2,1)S(1)}, f32[512,128]{1,0:T(8,128)S(1)}, f32[512,512]{1,0:T(8,128)S(1)}, bf16[512,512]{1,0:T(8,128)(2,1)S(1)}, bf16[512,512]{1,0:T(8,128)(2,1)S(1)}) custom-call(f32[2]{0:T(128)S(1)} %copy-done.15, f32[2]{0:T(128)S(1)} %collective-permute-done.8.refs_1_, f32[2]{0:T(128)S(1)} %collective-permute-done.9.refs_2_, ...), custom_call_target="tpu_custom_call" | custom-call | tf_op jit(solution)/shard_map/prepare/pallas_call | solution.py:511
  80.5 2.0 %copy-done.1 = bf16[8,512,512]{2,1,0:T(8,128)(2,1)} copy-done((bf16[8,512,512]{2,1,0:T(8,128)(2,1)}, bf16[8,512,512]{2,1,0:T(8,128)(2,1)S(1)}, u32[]{:S(2)}) %copy-start.1) | copy-done | bytes 4194328
  82.5 1.1 copy-done.4
  85.2 2.5 %all-to-all-done.1 = bf16[256,40,128]{2,1,0:T(8,128)(2,1)S(1)} async-done(((bf16[256,40,128]{2,1,0:T(8,128)(2,1)}), bf16[256,40,128]{2,1,0:T(8,128)(2,1)S(1)}, u32[]{:S(2)}, u32[]{:S(2)}) %all-to-all-start.1) | async-done | bytes 2621472 | tf_op jit(solution)/shard_map/all_to_all | solution.py:496
  87.7 1.8 plan.1
  90.7 20.3 %conditional.1 = (bf16[6,4,40,128]{3,2,1,0:T(8,128)(2,1)}, bf16[6,4,40,128]{3,2,1,0:T(8,128)(2,1)}, bf16[6,4,40,128]{3,2,1,0:T(8,128)(2,1)}, bf16[6,4,40,128]{3,...) conditional(s32[]{:T(128)} %bitcast.22, ...), branch_computations={%region_1.0_spmd, %region_2.0_spmd} | conditional | bytes 10485832 | solution.py:564
  91.0 1.8 collective-permute-start.2
  93.5 2.1 %collective-permute-start.4 = (bf16[6,4,40,128]{3,2,1,0:T(8,128)(2,1)S(1)}, bf16[6,4,40,128]{3,2,1,0:T(8,128)(2,1)}, u32[]{:S(2)}, u32[]{:S(2)}) collective-permute-start(bf16[6,4,40,128]{3,2,1,0:T(8,128)(2,1)S(1)} %get-tuple-element.37), channel_id=1, source_target_pairs={{0,196},{4,192},{8,204},{12,200},{16,212},{20,208},{24,220},{28,21... | collective-permute-start | bytes 737288 | tf_op jit(solution)/shard_map/cond/branch_1_fun/ppermute | solution.py:461
  95.7 1.2 collective-permute-start.5
  96.9 3.0 %collective-permute-done.1 = bf16[6,4,40,128]{3,2,1,0:T(8,128)(2,1)} collective-permute-done((bf16[6,4,40,128]{3,2,1,0:T(8,128)(2,1)S(1)}, bf16[6,4,40,128]{3,2,1,0:T(8,128)(2,1)}, u32[]{:S(2)}, u32[]{:S(2)}) %collective-permute-start.1) | collective-permute-done | bytes 245792 | tf_op jit(solution)/shard_map/cond/branch_1_fun/ppermute | solution.py:461
  99.8 4.3 %collective-permute-done.2 = bf16[6,4,40,128]{3,2,1,0:T(8,128)(2,1)} collective-permute-done((bf16[6,4,40,128]{3,2,1,0:T(8,128)(2,1)S(1)}, bf16[6,4,40,128]{3,2,1,0:T(8,128)(2,1)}, u32[]{:S(2)}, u32[]{:S(2)}) %collective-permute-start.2) | collective-permute-done | bytes 245792 | tf_op jit(solution)/shard_map/cond/branch_1_fun/ppermute | solution.py:461
  104.9 2.1 %collective-permute-done.4 = bf16[6,4,40,128]{3,2,1,0:T(8,128)(2,1)} collective-permute-done((bf16[6,4,40,128]{3,2,1,0:T(8,128)(2,1)S(1)}, bf16[6,4,40,128]{3,2,1,0:T(8,128)(2,1)}, u32[]{:S(2)}, u32[]{:S(2)}) %collective-permute-start.4) | collective-permute-done | bytes 245792 | tf_op jit(solution)/shard_map/cond/branch_1_fun/ppermute | solution.py:461
  107.0 1.9 %collective-permute-done.6 = bf16[6,4,40,128]{3,2,1,0:T(8,128)(2,1)} collective-permute-done((bf16[6,4,40,128]{3,2,1,0:T(8,128)(2,1)S(1)}, bf16[6,4,40,128]{3,2,1,0:T(8,128)(2,1)}, u32[]{:S(2)}, u32[]{:S(2)}) %collective-permute-start.6) | collective-permute-done | bytes 245792 | tf_op jit(solution)/shard_map/cond/branch_1_fun/ppermute | solution.py:461
  108.9 1.8 collective-permute-done.7
  111.0 0.9 copy-done.17
  112.0 2.2 %copy-done.2 = bf16[8,512,512]{2,1,0:T(8,128)(2,1)S(1)} copy-done((bf16[8,512,512]{2,1,0:T(8,128)(2,1)S(1)}, bf16[8,512,512]{2,1,0:T(8,128)(2,1)}, u32[]{:S(2)}) %copy-start.2) | copy-done | bytes 4194328
  114.1 1.2 copy-done.5
  115.4 1.0 copy-done.9
  116.4 12.5 %attend.1 = (bf16[128,640]{1,0:T(8,128)(2,1)S(1)}, bf16[128,640]{1,0:T(8,128)(2,1)}, bf16[128,640]{1,0:T(8,128)(2,1)}, bf16[128,640]{1,0:T(8,128)(2,1)}) custom-call(bf16[64,4,40,128]{3,2,1,0:T(8,128)(2,1)S(1)} %bitcast.39, bf16[6,4,40,128]{3,2,1,0:T(8,128)(2,1)} %get-tuple-element.83.refs_1_, bf16[6,4,40,128]{3,2,1,0:T(8,128)(2,1)} %get-tuple-element.84.refs_2_, ...), custom_call_target="tpu_custom_call" | custom-call | tf_op jit(solution)/shard_map/attend/pallas_call | solution.py:583
  130.1 1.5 collective-permute-start.15
  131.6 2.7 %collective-permute-start.16 = (bf16[128,640]{1,0:T(8,128)(2,1)}, bf16[128,640]{1,0:T(8,128)(2,1)S(1)}, u32[]{:S(2)}, u32[]{:S(2)}) collective-permute-start(bf16[128,640]{1,0:T(8,128)(2,1)} %get-tuple-element.99), channel_id=1, source_target_pairs={{0,3},{1,2},{2,1},{3,0},{4,7},{5,6},{6,5},{7,4},{8,11},{9,10},{10,... | collective-permute-start | bytes 491528 | tf_op jit(solution)/shard_map/ppermute | solution.py:461
  134.3 2.6 %collective-permute-done.14.r1 = bf16[128,640]{1,0:T(8,128)(2,1)S(1)} collective-permute-done((bf16[128,640]{1,0:T(8,128)(2,1)}, bf16[128,640]{1,0:T(8,128)(2,1)S(1)}, u32[]{:S(2)}, u32[]{:S(2)}) %collective-permute-start.14) | collective-permute-done | bytes 163872 | tf_op jit(solution)/shard_map/ppermute | solution.py:461
  136.8 2.5 %collective-permute-done.15.r2 = bf16[128,640]{1,0:T(8,128)(2,1)S(1)} collective-permute-done((bf16[128,640]{1,0:T(8,128)(2,1)}, bf16[128,640]{1,0:T(8,128)(2,1)S(1)}, u32[]{:S(2)}, u32[]{:S(2)}) %collective-permute-start.15) | collective-permute-done | bytes 163872 | tf_op jit(solution)/shard_map/ppermute | solution.py:461
  139.3 2.4 %collective-permute-done.16.r3 = bf16[128,640]{1,0:T(8,128)(2,1)S(1)} collective-permute-done((bf16[128,640]{1,0:T(8,128)(2,1)}, bf16[128,640]{1,0:T(8,128)(2,1)S(1)}, u32[]{:S(2)}, u32[]{:S(2)}) %collective-permute-start.16) | collective-permute-done | bytes 163872 | tf_op jit(solution)/shard_map/ppermute | solution.py:461
  141.8 1.0 copy-done.7
  144.6 1.4 finish.1
  146.2 4.1 %collective-permute-start.18 = (f32[256,128]{1,0:T(8,128)S(1)}, f32[256,128]{1,0:T(8,128)S(1)}, u32[]{:S(2)}, u32[]{:S(2)}) collective-permute-start(f32[256,128]{1,0:T(8,128)S(1)} %get-tuple-element.103), channel_id=1, source_target_pairs={{0,2},{1,3},{2,0},{3,1},{4,6},{5,7},{6,4},{7,5},{8,10},{9,11},{10,... | collective-permute-start | bytes 393224 | tf_op jit(solution)/shard_map/ppermute | solution.py:461
  150.9 1.4 collective-permute-done.17
  152.3 3.4 %collective-permute-done.18 = f32[256,128]{1,0:T(8,128)S(1)} collective-permute-done((f32[256,128]{1,0:T(8,128)S(1)}, f32[256,128]{1,0:T(8,128)S(1)}, u32[]{:S(2)}, u32[]{:S(2)}) %collective-permute-start.18) | collective-permute-done | bytes 131104 | tf_op jit(solution)/shard_map/ppermute | solution.py:461
  155.8 1.7 collective-permute-done.19
  157.6 1.2 collective-permute-start.21
  159.5 3.1 %collective-permute-done.21 = f32[128,128]{1,0:T(8,128)S(1)} collective-permute-done((f32[128,128]{1,0:T(8,128)S(1)}, f32[128,128]{1,0:T(8,128)S(1)}, u32[]{:S(2)}, u32[]{:S(2)}) %collective-permute-start.21) | collective-permute-done | bytes 65568 | tf_op jit(solution)/shard_map/ppermute | solution.py:461
  163.8 3.4 %collective-permute-start.24 = (f32[128,128]{1,0:T(8,128)S(1)}, f32[128,128]{1,0:T(8,128)S(1)}, u32[]{:S(2)}, u32[]{:S(2)}) collective-permute-start(f32[128,128]{1,0:T(8,128)S(1)} %add_add_fusion.1), channel_id=1, source_target_pairs={{0,32},{4,36},{8,40},{12,44},{16,48},{20,52},{24,56},{28,60},{32,0... | collective-permute-start | bytes 196616 | tf_op jit(solution)/shard_map/ppermute | solution.py:461
  167.2 2.6 %collective-permute-start.25 = (f32[128,128]{1,0:T(8,128)S(1)}, f32[128,128]{1,0:T(8,128)S(1)}, u32[]{:S(2)}, u32[]{:S(2)}) collective-permute-start(f32[128,128]{1,0:T(8,128)S(1)} %add_add_fusion.1), channel_id=1, source_target_pairs={{0,48},{4,52},{8,56},{12,60},{16,32},{20,36},{24,40},{28,44},{32,1... | collective-permute-start | bytes 196616 | tf_op jit(solution)/shard_map/ppermute | solution.py:461
  170.3 1.9 %collective-permute-done.24 = f32[128,128]{1,0:T(8,128)S(1)} collective-permute-done((f32[128,128]{1,0:T(8,128)S(1)}, f32[128,128]{1,0:T(8,128)S(1)}, u32[]{:S(2)}, u32[]{:S(2)}) %collective-permute-start.24) | collective-permute-done | bytes 65568 | tf_op jit(solution)/shard_map/ppermute | solution.py:461
  172.2 4.2 %collective-permute-done.25 = f32[128,128]{1,0:T(8,128)S(1)} collective-permute-done((f32[128,128]{1,0:T(8,128)S(1)}, f32[128,128]{1,0:T(8,128)S(1)}, u32[]{:S(2)}, u32[]{:S(2)}) %collective-permute-start.25) | collective-permute-done | bytes 65568 | tf_op jit(solution)/shard_map/ppermute | solution.py:461
  176.5 2.5 %collective-permute-start.27 = (f32[128,128]{1,0:T(8,128)S(1)}, f32[128,128]{1,0:T(8,128)S(1)}, u32[]{:S(2)}, u32[]{:S(2)}) collective-permute-start(f32[128,128]{1,0:T(8,128)S(1)} %add_add_fusion), channel_id=1, source_target_pairs={{0,128},{4,132},{8,136},{12,140},{16,144},{20,148},{24,152},{28,15... | collective-permute-start | bytes 196616 | tf_op jit(solution)/shard_map/ppermute | solution.py:461
  179.0 2.2 %collective-permute-start.28 = (f32[128,128]{1,0:T(8,128)S(1)}, f32[128,128]{1,0:T(8,128)S(1)}, u32[]{:S(2)}, u32[]{:S(2)}) collective-permute-start(f32[128,128]{1,0:T(8,128)S(1)} %add_add_fusion), channel_id=1, source_target_pairs={{0,192},{4,196},{8,200},{12,204},{16,208},{20,212},{24,216},{28,22... | collective-permute-start | bytes 196616 | tf_op jit(solution)/shard_map/ppermute | solution.py:461
  182.8 1.7 collective-permute-done.28
  (80 shorter events, 14.2 us)
Async XLA Ops:
  6.1 1.5 copy-start
  7.6 14.4 %copy-start.19 = (bf16[128,512]{1,0:T(8,128)(2,1)S(1)}, bf16[128,512]{1,0:T(8,128)(2,1)}, u32[]{:S(2)}) copy-start(bf16[128,512]{1,0:T(8,128)(2,1)} %param.24) | copy-start | bytes 393220
  7.6 14.5 %copy-start.20 = (bf16[512,128]{1,0:T(8,128)(2,1)S(1)}, bf16[512,128]{1,0:T(8,128)(2,1)}, u32[]{:S(2)}) copy-start(bf16[512,128]{1,0:T(8,128)(2,1)} %param.22) | copy-start | bytes 393220
  7.6 20.4 %copy-start.15 = (f32[2]{0:T(128)S(1)}, f32[2]{0:T(128)}, u32[]{:S(2)}) copy-start(f32[2]{0:T(128)} %refs_0_.1) | copy-start | bytes 28
  7.6 69.2 %copy-start.3 = (bf16[512,512]{1,0:T(8,128)(2,1)S(1)}, bf16[512,512]{1,0:T(8,128)(2,1)}, u32[]{:S(2)}) copy-start(bf16[512,512]{1,0:T(8,128)(2,1)} %lat.1) | copy-start | bytes 1572868
  7.6 80.1 %all-to-all-start.1 = ((bf16[256,40,128]{2,1,0:T(8,128)(2,1)}), bf16[256,40,128]{2,1,0:T(8,128)(2,1)S(1)}, u32[]{:S(2)}, u32[]{:S(2)}) async-start(bf16[256,40,128]{2,1,0:T(8,128)(2,1)} %bitcast.40), calls=%async_computation.1 | async-start | bytes 5242880 | tf_op jit(solution)/shard_map/all_to_all | solution.py:496
  23.2 53.6 %collective-permute-start.11 = (bf16[512,512]{1,0:T(8,128)(2,1)S(1)}, bf16[512,512]{1,0:T(8,128)(2,1)S(1)}, u32[]{:S(2)}, u32[]{:S(2)}) collective-permute-start(bf16[512,512]{1,0:T(8,128)(2,1)S(1)} %pad_maximum_fusion.refs_4_), channel_id=1, source_target_pairs={{0,1},{1,0},{2,3},{3,2},{4,5},{5,4},{6,7},{7,6},{8,9},{9,8},{10,11... | collective-permute-start | bytes 1572872 | tf_op jit(solution)/shard_map/ppermute | solution.py:461
  24.8 52.0 %collective-permute-start.12 = (bf16[512,512]{1,0:T(8,128)(2,1)S(1)}, bf16[512,512]{1,0:T(8,128)(2,1)S(1)}, u32[]{:S(2)}, u32[]{:S(2)}) collective-permute-start(bf16[512,512]{1,0:T(8,128)(2,1)S(1)} %pad_maximum_fusion.refs_4_), channel_id=1, source_target_pairs={{0,2},{1,3},{2,0},{3,1},{4,6},{5,7},{6,4},{7,5},{8,10},{9,11},{10,... | collective-permute-start | bytes 1572872 | tf_op jit(solution)/shard_map/ppermute | solution.py:461
  27.5 49.3 %collective-permute-start.13 = (bf16[512,512]{1,0:T(8,128)(2,1)S(1)}, bf16[512,512]{1,0:T(8,128)(2,1)S(1)}, u32[]{:S(2)}, u32[]{:S(2)}) collective-permute-start(bf16[512,512]{1,0:T(8,128)(2,1)S(1)} %pad_maximum_fusion.refs_4_), channel_id=1, source_target_pairs={{0,3},{1,2},{2,1},{3,0},{4,7},{5,6},{6,5},{7,4},{8,11},{9,10},{10,... | collective-permute-start | bytes 1572872 | tf_op jit(solution)/shard_map/ppermute | solution.py:461
  28.0 43.8 %collective-permute-start.10 = (f32[2]{0:T(128)S(1)}, f32[2]{0:T(128)S(1)}, u32[]{:S(2)}, u32[]{:S(2)}) collective-permute-start(f32[2]{0:T(128)S(1)} %copy-done.15), channel_id=1, source_target_pairs={{0,3},{1,2},{2,1},{3,0},{4,7},{5,6},{6,5},{7,4},{8,11},{9,10},{10,... | collective-permute-start | bytes 32 | tf_op jit(solution)/shard_map/ppermute | solution.py:461
  30.7 41.0 %collective-permute-start.8 = (f32[2]{0:T(128)S(1)}, f32[2]{0:T(128)S(1)}, u32[]{:S(2)}, u32[]{:S(2)}) collective-permute-start(f32[2]{0:T(128)S(1)} %copy-done.15), channel_id=1, source_target_pairs={{0,1},{1,0},{2,3},{3,2},{4,5},{5,4},{6,7},{7,6},{8,9},{9,8},{10,11... | collective-permute-start | bytes 32 | tf_op jit(solution)/shard_map/ppermute | solution.py:461
  30.7 60.0 %copy-start.18 = (s32[8192]{0:T(1024)S(1)}, s32[8192]{0:T(1024)}, u32[]{:S(2)}) copy-start(s32[8192]{0:T(1024)} %param.16) | copy-start | bytes 98308
  30.7 60.0 %copy-start.21 = (s32[64,16]{0,1:T(8,128)S(1)}, s32[64,16]{0,1:T(8,128)}, u32[]{:S(2)}) copy-start(s32[64,16]{0,1:T(8,128)} %param.18) | copy-start | bytes 12292
  30.7 60.0 %copy-start.22 = (s32[64,1]{0,1:T(1,128)S(1)}, s32[64,1]{0,1:T(1,128)}, u32[]{:S(2)}) copy-start(s32[64,1]{0,1:T(1,128)} %param.17) | copy-start | bytes 772
  71.7 5.0 %collective-permute-start.9 = (f32[2]{0:T(128)S(1)}, f32[2]{0:T(128)S(1)}, u32[]{:S(2)}, u32[]{:S(2)}) collective-permute-start(f32[2]{0:T(128)S(1)} %copy-done.15), channel_id=1, source_target_pairs={{0,2},{1,3},{2,0},{3,1},{4,6},{5,7},{6,4},{7,5},{8,10},{9,11},{10,... | collective-permute-start | bytes 32 | tf_op jit(solution)/shard_map/ppermute | solution.py:461
  80.5 2.0 %copy-start.1 = (bf16[8,512,512]{2,1,0:T(8,128)(2,1)}, bf16[8,512,512]{2,1,0:T(8,128)(2,1)S(1)}, u32[]{:S(2)}) copy-start(bf16[8,512,512]{2,1,0:T(8,128)(2,1)S(1)} %get-tuple-element.92.refs_10_) | copy-start | bytes 12582916
  82.5 1.1 copy-start.4
  87.7 3.0 %copy-start.16 = (bf16[8192,128]{1,0:T(8,128)(2,1)S(1)}, bf16[8192,128]{1,0:T(8,128)(2,1)}, u32[]{:S(2)}) copy-start(bf16[8192,128]{1,0:T(8,128)(2,1)} %param.15) | copy-start | bytes 6291460
  90.8 4.9 %collective-permute-start = (bf16[6,4,40,128]{3,2,1,0:T(8,128)(2,1)S(1)}, bf16[6,4,40,128]{3,2,1,0:T(8,128)(2,1)}, u32[]{:S(2)}, u32[]{:S(2)}) collective-permute-start(bf16[6,4,40,128]{3,2,1,0:T(8,128)(2,1)S(1)} %get-tuple-element.32), channel_id=1, source_target_pairs={{0,4},{4,0},{8,12},{12,8},{16,20},{20,16},{24,28},{28,24},{32,36},... | collective-permute-start | bytes 737288 | tf_op jit(solution)/shard_map/cond/branch_1_fun/ppermute | solution.py:461
  90.9 9.0 %collective-permute-start.1 = (bf16[6,4,40,128]{3,2,1,0:T(8,128)(2,1)S(1)}, bf16[6,4,40,128]{3,2,1,0:T(8,128)(2,1)}, u32[]{:S(2)}, u32[]{:S(2)}) collective-permute-start(bf16[6,4,40,128]{3,2,1,0:T(8,128)(2,1)S(1)} %get-tuple-element.34), channel_id=1, source_target_pairs={{0,64},{4,68},{8,72},{12,76},{16,80},{20,84},{24,88},{28,92},{32,9... | collective-permute-start | bytes 737288 | tf_op jit(solution)/shard_map/cond/branch_1_fun/ppermute | solution.py:461
  91.0 13.2 %collective-permute-start.2 = (bf16[6,4,40,128]{3,2,1,0:T(8,128)(2,1)S(1)}, bf16[6,4,40,128]{3,2,1,0:T(8,128)(2,1)}, u32[]{:S(2)}, u32[]{:S(2)}) collective-permute-start(bf16[6,4,40,128]{3,2,1,0:T(8,128)(2,1)S(1)} %get-tuple-element.35), channel_id=1, source_target_pairs={{0,68},{4,64},{8,76},{12,72},{16,84},{20,80},{24,92},{28,88},{32,1... | collective-permute-start | bytes 737288 | tf_op jit(solution)/shard_map/cond/branch_1_fun/ppermute | solution.py:461
  92.7 12.1 %collective-permute-start.3 = (bf16[6,4,40,128]{3,2,1,0:T(8,128)(2,1)S(1)}, bf16[6,4,40,128]{3,2,1,0:T(8,128)(2,1)}, u32[]{:S(2)}, u32[]{:S(2)}) collective-permute-start(bf16[6,4,40,128]{3,2,1,0:T(8,128)(2,1)S(1)} %get-tuple-element.36), channel_id=1, source_target_pairs={{0,192},{4,196},{8,200},{12,204},{16,208},{20,212},{24,216},{28,22... | collective-permute-start | bytes 737288 | tf_op jit(solution)/shard_map/cond/branch_1_fun/ppermute | solution.py:461
  93.5 13.4 %collective-permute-start.4 = (bf16[6,4,40,128]{3,2,1,0:T(8,128)(2,1)S(1)}, bf16[6,4,40,128]{3,2,1,0:T(8,128)(2,1)}, u32[]{:S(2)}, u32[]{:S(2)}) collective-permute-start(bf16[6,4,40,128]{3,2,1,0:T(8,128)(2,1)S(1)} %get-tuple-element.37), channel_id=1, source_target_pairs={{0,196},{4,192},{8,204},{12,200},{16,212},{20,208},{24,220},{28,21... | collective-permute-start | bytes 737288 | tf_op jit(solution)/shard_map/cond/branch_1_fun/ppermute | solution.py:461
  95.7 11.3 %collective-permute-start.5 = (bf16[6,4,40,128]{3,2,1,0:T(8,128)(2,1)S(1)}, bf16[6,4,40,128]{3,2,1,0:T(8,128)(2,1)}, u32[]{:S(2)}, u32[]{:S(2)}) collective-permute-start(bf16[6,4,40,128]{3,2,1,0:T(8,128)(2,1)S(1)} %get-tuple-element.38), channel_id=1, source_target_pairs={{0,8},{4,12},{8,0},{12,4},{16,24},{20,28},{24,16},{28,20},{32,40},... | collective-permute-start | bytes 737288 | tf_op jit(solution)/shard_map/cond/branch_1_fun/ppermute | solution.py:461
  99.8 9.1 %collective-permute-start.6 = (bf16[6,4,40,128]{3,2,1,0:T(8,128)(2,1)S(1)}, bf16[6,4,40,128]{3,2,1,0:T(8,128)(2,1)}, u32[]{:S(2)}, u32[]{:S(2)}) collective-permute-start(bf16[6,4,40,128]{3,2,1,0:T(8,128)(2,1)S(1)} %get-tuple-element.39), channel_id=1, source_target_pairs={{0,12},{4,8},{8,4},{12,0},{16,28},{20,24},{24,20},{28,16},{32,44},... | collective-permute-start | bytes 737288 | tf_op jit(solution)/shard_map/cond/branch_1_fun/ppermute | solution.py:461
  104.1 6.6 %collective-permute-start.7 = (bf16[2,4,40,128]{3,2,1,0:T(8,128)(2,1)S(1)}, bf16[2,4,40,128]{3,2,1,0:T(8,128)(2,1)}, u32[]{:S(2)}, u32[]{:S(2)}) collective-permute-start(bf16[2,4,40,128]{3,2,1,0:T(8,128)(2,1)S(1)} %get-tuple-element.40), channel_id=1, source_target_pairs={{0,128},{4,132},{8,136},{12,140},{16,144},{20,148},{24,152},{28,15... | collective-permute-start | bytes 245768 | tf_op jit(solution)/shard_map/cond/branch_1_fun/ppermute | solution.py:461
  111.0 0.9 copy-start.17
  111.9 2.2 %copy-start.2 = (bf16[8,512,512]{2,1,0:T(8,128)(2,1)S(1)}, bf16[8,512,512]{2,1,0:T(8,128)(2,1)}, u32[]{:S(2)}) copy-start(bf16[8,512,512]{2,1,0:T(8,128)(2,1)} %copy-done.1) | copy-start | bytes 12582916
  114.1 1.2 copy-start.5
  115.4 1.0 copy-start.9
  116.4 25.4 %copy-start.12 = (bf16[512,128]{1,0:T(8,128)(2,1)S(1)}, bf16[512,128]{1,0:T(8,128)(2,1)}, u32[]{:S(2)}) copy-start(bf16[512,128]{1,0:T(8,128)(2,1)} %w_inc.1) | copy-start | bytes 393220
  116.4 25.4 %copy-start.14 = (f32[512]{0:T(512)S(1)}, f32[512]{0:T(512)}, u32[]{:S(2)}) copy-start(f32[512]{0:T(512)} %param.25) | copy-start | bytes 6148
  129.6 7.3 %collective-permute-start.14 = (bf16[128,640]{1,0:T(8,128)(2,1)}, bf16[128,640]{1,0:T(8,128)(2,1)S(1)}, u32[]{:S(2)}, u32[]{:S(2)}) collective-permute-start(bf16[128,640]{1,0:T(8,128)(2,1)} %get-tuple-element.97), channel_id=1, source_target_pairs={{0,1},{1,0},{2,3},{3,2},{4,5},{5,4},{6,7},{7,6},{8,9},{9,8},{10,11... | collective-permute-start | bytes 491528 | tf_op jit(solution)/shard_map/ppermute | solution.py:461
  130.1 9.2 %collective-permute-start.15 = (bf16[128,640]{1,0:T(8,128)(2,1)}, bf16[128,640]{1,0:T(8,128)(2,1)S(1)}, u32[]{:S(2)}, u32[]{:S(2)}) collective-permute-start(bf16[128,640]{1,0:T(8,128)(2,1)} %get-tuple-element.98), channel_id=1, source_target_pairs={{0,2},{1,3},{2,0},{3,1},{4,6},{5,7},{6,4},{7,5},{8,10},{9,11},{10,... | collective-permute-start | bytes 491528 | tf_op jit(solution)/shard_map/ppermute | solution.py:461
  131.6 10.2 %collective-permute-start.16 = (bf16[128,640]{1,0:T(8,128)(2,1)}, bf16[128,640]{1,0:T(8,128)(2,1)S(1)}, u32[]{:S(2)}, u32[]{:S(2)}) collective-permute-start(bf16[128,640]{1,0:T(8,128)(2,1)} %get-tuple-element.99), channel_id=1, source_target_pairs={{0,3},{1,2},{2,1},{3,0},{4,7},{5,6},{6,5},{7,4},{8,11},{9,10},{10,... | collective-permute-start | bytes 491528 | tf_op jit(solution)/shard_map/ppermute | solution.py:461
  141.8 1.0 copy-start.7
  146.1 6.3 %collective-permute-start.17 = (f32[256,128]{1,0:T(8,128)S(1)}, f32[256,128]{1,0:T(8,128)S(1)}, u32[]{:S(2)}, u32[]{:S(2)}) collective-permute-start(f32[256,128]{1,0:T(8,128)S(1)} %get-tuple-element.102), channel_id=1, source_target_pairs={{0,1},{1,0},{2,3},{3,2},{4,5},{5,4},{6,7},{7,6},{8,9},{9,8},{10,11... | collective-permute-start | bytes 393224 | tf_op jit(solution)/shard_map/ppermute | solution.py:461
  146.2 9.6 %collective-permute-start.18 = (f32[256,128]{1,0:T(8,128)S(1)}, f32[256,128]{1,0:T(8,128)S(1)}, u32[]{:S(2)}, u32[]{:S(2)}) collective-permute-start(f32[256,128]{1,0:T(8,128)S(1)} %get-tuple-element.103), channel_id=1, source_target_pairs={{0,2},{1,3},{2,0},{3,1},{4,6},{5,7},{6,4},{7,5},{8,10},{9,11},{10,... | collective-permute-start | bytes 393224 | tf_op jit(solution)/shard_map/ppermute | solution.py:461
  150.3 7.2 %collective-permute-start.19 = (f32[256,128]{1,0:T(8,128)S(1)}, f32[256,128]{1,0:T(8,128)S(1)}, u32[]{:S(2)}, u32[]{:S(2)}) collective-permute-start(f32[256,128]{1,0:T(8,128)S(1)} %get-tuple-element.104), channel_id=1, source_target_pairs={{0,3},{1,2},{2,1},{3,0},{4,7},{5,6},{6,5},{7,4},{8,11},{9,10},{10,... | collective-permute-start | bytes 393224 | tf_op jit(solution)/shard_map/ppermute | solution.py:461
  157.5 2.0 %collective-permute-start.20 = (f32[128,128]{1,0:T(8,128)S(1)}, f32[128,128]{1,0:T(8,128)S(1)}, u32[]{:S(2)}, u32[]{:S(2)}) collective-permute-start(f32[128,128]{1,0:T(8,128)S(1)} %get-tuple-element.112), channel_id=1, source_target_pairs={{0,4},{4,0},{8,12},{12,8},{16,20},{20,16},{24,28},{28,24},{32,36},... | collective-permute-start | bytes 196616 | tf_op jit(solution)/shard_map/ppermute | solution.py:461
  157.6 4.9 %collective-permute-start.21 = (f32[128,128]{1,0:T(8,128)S(1)}, f32[128,128]{1,0:T(8,128)S(1)}, u32[]{:S(2)}, u32[]{:S(2)}) collective-permute-start(f32[128,128]{1,0:T(8,128)S(1)} %get-tuple-element.112), channel_id=1, source_target_pairs={{0,8},{4,12},{8,0},{12,4},{16,24},{20,28},{24,16},{28,20},{32,40},... | collective-permute-start | bytes 196616 | tf_op jit(solution)/shard_map/ppermute | solution.py:461
  158.8 4.3 %collective-permute-start.22 = (f32[128,128]{1,0:T(8,128)S(1)}, f32[128,128]{1,0:T(8,128)S(1)}, u32[]{:S(2)}, u32[]{:S(2)}) collective-permute-start(f32[128,128]{1,0:T(8,128)S(1)} %get-tuple-element.112), channel_id=1, source_target_pairs={{0,12},{4,8},{8,4},{12,0},{16,28},{20,24},{24,20},{28,16},{32,44},... | collective-permute-start | bytes 196616 | tf_op jit(solution)/shard_map/ppermute | solution.py:461
  163.1 7.2 %collective-permute-start.23 = (f32[128,128]{1,0:T(8,128)S(1)}, f32[128,128]{1,0:T(8,128)S(1)}, u32[]{:S(2)}, u32[]{:S(2)}) collective-permute-start(f32[128,128]{1,0:T(8,128)S(1)} %add_add_fusion.1), channel_id=1, source_target_pairs={{0,16},{4,20},{8,24},{12,28},{16,0},{20,4},{24,8},{28,12},{32,48},... | collective-permute-start | bytes 196616 | tf_op jit(solution)/shard_map/ppermute | solution.py:461
  163.8 8.4 %collective-permute-start.24 = (f32[128,128]{1,0:T(8,128)S(1)}, f32[128,128]{1,0:T(8,128)S(1)}, u32[]{:S(2)}, u32[]{:S(2)}) collective-permute-start(f32[128,128]{1,0:T(8,128)S(1)} %add_add_fusion.1), channel_id=1, source_target_pairs={{0,32},{4,36},{8,40},{12,44},{16,48},{20,52},{24,56},{28,60},{32,0... | collective-permute-start | bytes 196616 | tf_op jit(solution)/shard_map/ppermute | solution.py:461
  167.2 9.3 %collective-permute-start.25 = (f32[128,128]{1,0:T(8,128)S(1)}, f32[128,128]{1,0:T(8,128)S(1)}, u32[]{:S(2)}, u32[]{:S(2)}) collective-permute-start(f32[128,128]{1,0:T(8,128)S(1)} %add_add_fusion.1), channel_id=1, source_target_pairs={{0,48},{4,52},{8,56},{12,60},{16,32},{20,36},{24,40},{28,44},{32,1... | collective-permute-start | bytes 196616 | tf_op jit(solution)/shard_map/ppermute | solution.py:461
  176.4 5.6 %collective-permute-start.26 = (f32[128,128]{1,0:T(8,128)S(1)}, f32[128,128]{1,0:T(8,128)S(1)}, u32[]{:S(2)}, u32[]{:S(2)}) collective-permute-start(f32[128,128]{1,0:T(8,128)S(1)} %add_add_fusion), channel_id=1, source_target_pairs={{0,64},{4,68},{8,72},{12,76},{16,80},{20,84},{24,88},{28,92},{32,9... | collective-permute-start | bytes 196616 | tf_op jit(solution)/shard_map/ppermute | solution.py:461
  176.5 6.2 %collective-permute-start.27 = (f32[128,128]{1,0:T(8,128)S(1)}, f32[128,128]{1,0:T(8,128)S(1)}, u32[]{:S(2)}, u32[]{:S(2)}) collective-permute-start(f32[128,128]{1,0:T(8,128)S(1)} %add_add_fusion), channel_id=1, source_target_pairs={{0,128},{4,132},{8,136},{12,140},{16,144},{20,148},{24,152},{28,15... | collective-permute-start | bytes 196616 | tf_op jit(solution)/shard_map/ppermute | solution.py:461
  179.0 5.5 %collective-permute-start.28 = (f32[128,128]{1,0:T(8,128)S(1)}, f32[128,128]{1,0:T(8,128)S(1)}, u32[]{:S(2)}, u32[]{:S(2)}) collective-permute-start(f32[128,128]{1,0:T(8,128)S(1)} %add_add_fusion), channel_id=1, source_target_pairs={{0,192},{4,196},{8,200},{12,204},{16,208},{20,212},{24,216},{28,22... | collective-permute-start | bytes 196616 | tf_op jit(solution)/shard_map/ppermute | solution.py:461
  (5 other events, 4.1 us)
